TPU v7x, 512 devices: a whole 4x4x16 slice. The times are simulated.
512 devices in a mesh: mode: 8 (over y_lo, x), slab: 64 (over z, y_hi, core).
Axes of the slice: x: 4, y: 4 (y_hi: 2, y_lo: 2; y = y_hi * 2 + y_lo), z: 16, core: 2. Of those that a mesh axis runs over, the one named last changes fastest.
Arguments:
- chaos_field: float32 [1024, 192, 1024], P('mode', 'slab'), may hold values from -4 to 4
- diffusivity: float32 [192, 1024], P('slab'), may hold values from 0.03 to 0.16
- growth_rate: float32 [192, 1024], P('slab'), may hold values from 0.3 to 3
- mode_table: int32 [1024, 8], replicated, may hold values from 0 to 2, as said below
- point_index: int32 [2048, 8], replicated, may hold values from 0 to 6
Outputs:
- final_field: float32 [1024, 192, 1024], P('mode', 'slab')
Inputs may be any that keep to these rules, and one draw needn't show every extreme that they name: `mode_table`: the rows are distinct multi-indices.
All inputs are finite; a program needn't handle non-finite values.
Results may differ from a plain program's by a relative error of at most 0.0035.
Values may be sent and summed in bfloat16 or wider, within the bound.
A program may use at most 64 MiB of HBM per device.

v0:
```python
import jax
import jax.numpy as jnp
from jax import lax
from jax.sharding import PartitionSpec as P

MODES = 1024
POINTS = 2048
NODES = 7
NY = 32
SWEEPS = 3
STEPS = 2


def with_halo(x, sides, width):
    for axis, dim in sides:
        count, length = (lax.axis_size(axis), x.shape[dim])
        up = [(i, (i + 1) % count) for i in range(count - 1)]
        down = [(j, i) for i, j in up]
        last = lax.slice_in_dim(x, length - width, length, axis=dim)
        leading = lax.slice_in_dim(x, 0, width, axis=dim)
        before = lax.ppermute(last, axis, up)
        after = lax.ppermute(leading, axis, down)
        x = jnp.concatenate([before, x, after], axis=dim)
    return x


def make_basis(mode_table, point_index):
    abscissa = (point_index.astype(jnp.float32) - (NODES - 1) / 2.0) * 0.32
    second = (abscissa * abscissa - 1.0) * 0.7071067811865476
    result = None
    for place in range(mode_table.shape[1]):
        degree = mode_table[None, :, place]
        factor = jnp.where(
            degree == 0,
            jnp.float32(1.0),
            jnp.where(degree == 1, abscissa[:, place : place + 1], second[:, place : place + 1]),
        )
        result = factor if result is None else result * factor
    return result


def sweep(extended, kappa_mid, size_y):
    middle = extended[:, 1:-1]
    cell_count = middle.shape[2]
    column = lax.broadcasted_iota(jnp.int32, (1, 1, cell_count), 2) % size_y
    x_pair = jnp.roll(middle, size_y, 2) + jnp.roll(middle, -size_y, 2)
    y_lower = jnp.where(column == 0, jnp.roll(middle, 1 - size_y, 2), jnp.roll(middle, 1, 2))
    y_upper = jnp.where(
        column == size_y - 1, jnp.roll(middle, size_y - 1, 2), jnp.roll(middle, -1, 2)
    )
    beside_all = x_pair + (y_lower + y_upper)
    beside_all = beside_all + extended[:, 2:] + extended[:, :-2]
    return middle + kappa_mid[None] * (beside_all - 6.0 * middle)


def per_device(chaos_field, diffusivity, growth_rate, mode_table, point_index):
    local_modes, planes, cell_count = chaos_field.shape
    groups = lax.axis_size("mode")
    cell_share = planes * cell_count // groups
    offset = lax.axis_index("mode") * cell_share
    growth_part = lax.dynamic_slice_in_dim(
        growth_rate.reshape(planes * cell_count), offset, cell_share, 0
    )
    forward_scale = 8.0 * MODES ** (-0.5)
    backward_scale = 1.4 * MODES**0.5 / POINTS
    basis_low = make_basis(mode_table, point_index).astype(jnp.bfloat16)
    current = chaos_field
    for outer_step in range(STEPS):
        for sweep_step in range(SWEEPS):
            extended = with_halo(current, (("slab", 1),), 1)
            current = sweep(extended, diffusivity, NY)
        flat_low = current.reshape(local_modes, planes * cell_count).astype(jnp.bfloat16)
        gathered = lax.all_to_all(flat_low, "mode", split_axis=1, concat_axis=0, tiled=True)
        values = jnp.dot(basis_low, gathered, preferred_element_type=jnp.float32) * forward_scale
        reaction = (0.5 * (growth_part[None] * values - values * values * values)).astype(
            jnp.bfloat16
        )
        increment = (
            lax.dot_general(
                basis_low, reaction, (((0,), (0,)), ((), ())), preferred_element_type=jnp.float32
            )
            * backward_scale
        )
        returned = lax.all_to_all(increment, "mode", split_axis=0, concat_axis=1, tiled=True)
        current = current + returned.reshape(local_modes, planes, cell_count)
    return current


def solution(mesh):
    return jax.shard_map(
        per_device,
        mesh=mesh,
        in_specs=(P("mode", "slab", None), P("slab", None), P("slab", None), P(), P()),
        out_specs=P("mode", "slab", None),
        check_vma=False,
    )
```

profile of v0, /device:TPU:129, one launch (start us, length us, event | category | flops | bytes accessed | tf_op | source)
XLA Modules:
  0.0 233.4 jit_solution(12994413020194682557)
XLA Ops:
  0.0 1.9 copy.23
  2.0 2.6 %collective-permute-start = (f32[128,1,1024]{0,2,1:T(8,128)S(1)}, f32[128,1,1024]{0,2,1:T(8,128)S(1)}, u32[]{:S(2)}, u32[]{:S(2)}) collective-permute-start(f32[128,1,1024]{0,2,1:T(8,128)S(1)} %get-tuple-element.107), channel_id=1, source_target_pairs={{1,0},{2,1},{3,2},{4,3},{5,4},{6,5},{7,6},{8,7},{9,8},{10,9},{11,1... | collective-permute-start | bytes 1572872 | tf_op jit(solution)/shard_map/ppermute | solution.py:22
  4.5 4.7 %collective-permute-start.1 = (f32[128,1,1024]{0,2,1:T(8,128)S(1)}, f32[128,1,1024]{0,2,1:T(8,128)S(1)}, u32[]{:S(2)}, u32[]{:S(2)}) collective-permute-start(f32[128,1,1024]{0,2,1:T(8,128)S(1)} %get-tuple-element.108), channel_id=1, source_target_pairs={{0,1},{1,2},{2,3},{3,4},{4,5},{5,6},{6,7},{7,8},{8,9},{9,10},{10,1... | collective-permute-start | bytes 1572872 | tf_op jit(solution)/shard_map/ppermute | solution.py:21
  9.8 0.2 fusion.112
  10.0 0.5 copy-done.2
  10.9 3.3 %collective-permute-done = f32[128,1,1024]{0,2,1:T(8,128)S(1)} collective-permute-done((f32[128,1,1024]{0,2,1:T(8,128)S(1)}, f32[128,1,1024]{0,2,1:T(8,128)S(1)}, u32[]{:S(2)}, u32[]{:S(2)}) %collective-permute-start) | collective-permute-done | bytes 524320 | tf_op jit(solution)/shard_map/ppermute | solution.py:22
  14.2 5.8 %collective-permute-done.1 = f32[128,1,1024]{0,2,1:T(8,128)S(1)} collective-permute-done((f32[128,1,1024]{0,2,1:T(8,128)S(1)}, f32[128,1,1024]{0,2,1:T(8,128)S(1)}, u32[]{:S(2)}, u32[]{:S(2)}) %collective-permute-start.1) | collective-permute-done | bytes 524320 | tf_op jit(solution)/shard_map/ppermute | solution.py:21
  20.0 2.5 %fusion.38 = f32[128,3,1024]{0,2,1:T(8,128)S(1)} fusion(f32[128,3,1024]{0,2,1:T(8,128)S(1)} %copy.23, f32[128,1,1024]{0,2,1:T(8,128)S(1)} %collective-permute-done.1, f32[128,1,1024]{0,2,1:T(8,128)S(1)} %collective-permute-done, f32[128,3,992]{0,2,1:T(8,128)S(1)} %get-tuple-element.104, f32[128,3,32]{0,2,1:T(8,128)S(1)} %get-tuple-element.106, ...), kind=kLoop, calls=%fused_computation.50 | loop fusion | flops 7471104 | bytes 13645824 | tf_op jit(solution)/shard_map/add | solution.py:53
  22.8 0.2 fusion.108
  23.0 2.8 %collective-permute-start.2 = (f32[128,1,1024]{0,2,1:T(8,128)S(1)}, f32[128,1,1024]{0,2,1:T(8,128)S(1)}, u32[]{:S(2)}, u32[]{:S(2)}) collective-permute-start(f32[128,1,1024]{0,2,1:T(8,128)S(1)} %get-tuple-element.93), channel_id=1, source_target_pairs={{1,0},{2,1},{3,2},{4,3},{5,4},{6,5},{7,6},{8,7},{9,8},{10,9},{11,1... | collective-permute-start | bytes 1572872 | tf_op jit(solution)/shard_map/ppermute | solution.py:22
  25.8 5.0 %collective-permute-start.3 = (f32[128,1,1024]{0,2,1:T(8,128)S(1)}, f32[128,1,1024]{0,2,1:T(8,128)S(1)}, u32[]{:S(2)}, u32[]{:S(2)}) collective-permute-start(f32[128,1,1024]{0,2,1:T(8,128)S(1)} %get-tuple-element.94), channel_id=1, source_target_pairs={{0,1},{1,2},{2,3},{3,4},{4,5},{5,6},{6,7},{7,8},{8,9},{9,10},{10,1... | collective-permute-start | bytes 1572872 | tf_op jit(solution)/shard_map/ppermute | solution.py:21
  30.9 0.2 fusion.105
  31.1 10.3 %collective-permute-done.2 = f32[128,1,1024]{0,2,1:T(8,128)S(1)} collective-permute-done((f32[128,1,1024]{0,2,1:T(8,128)S(1)}, f32[128,1,1024]{0,2,1:T(8,128)S(1)}, u32[]{:S(2)}, u32[]{:S(2)}) %collective-permute-start.2) | collective-permute-done | bytes 524320 | tf_op jit(solution)/shard_map/ppermute | solution.py:22
  41.4 2.5 %fusion.33 = f32[128,3,1024]{0,2,1:T(8,128)S(1)} fusion(f32[128,3,1024]{0,2,1:T(8,128)S(1)} %fusion.38, f32[128,1,1024]{0,2,1:T(8,128)S(1)} %collective-permute-done.3, f32[128,1,1024]{0,2,1:T(8,128)S(1)} %collective-permute-done.2, f32[128,3,992]{0,2,1:T(8,128)S(1)} %get-tuple-element.90, f32[128,3,32]{0,2,1:T(8,128)S(1)} %get-tuple-element.92, ...), kind=kLoop, calls=%fused_computation.43 | loop fusion | flops 7471104 | bytes 13645824 | tf_op jit(solution)/shard_map/add | solution.py:53
  44.4 1.9 collective-permute-start.4
  46.4 5.1 %collective-permute-start.5 = (f32[128,1,1024]{0,2,1:T(8,128)S(1)}, f32[128,1,1024]{0,2,1:T(8,128)S(1)}, u32[]{:S(2)}, u32[]{:S(2)}) collective-permute-start(f32[128,1,1024]{0,2,1:T(8,128)S(1)} %get-tuple-element.80), channel_id=1, source_target_pairs={{0,1},{1,2},{2,3},{3,4},{4,5},{5,6},{6,7},{7,8},{8,9},{9,10},{10,1... | collective-permute-start | bytes 1572872 | tf_op jit(solution)/shard_map/ppermute | solution.py:21
  51.5 0.2 fusion.103
  51.8 10.3 %collective-permute-done.4 = f32[128,1,1024]{0,2,1:T(8,128)S(1)} collective-permute-done((f32[128,1,1024]{0,2,1:T(8,128)S(1)}, f32[128,1,1024]{0,2,1:T(8,128)S(1)}, u32[]{:S(2)}, u32[]{:S(2)}) %collective-permute-start.4) | collective-permute-done | bytes 524320 | tf_op jit(solution)/shard_map/ppermute | solution.py:22
  62.1 3.2 %fusion.75 = (bf16[128,3,1024]{0,2,1:T(8,128)(2,1)}, f32[128,3,1024]{0,2,1:T(8,128)S(1)}) fusion(f32[128,3,1024]{0,2,1:T(8,128)S(1)} %fusion.33, f32[128,1,1024]{0,2,1:T(8,128)S(1)} %collective-permute-done.5, f32[128,1,1024]{0,2,1:T(8,128)S(1)} %collective-permute-done.4, f32[128,3,1]{0,2,1:T(1,128)S(1)} %get-tuple-element.76, ...), kind=kLoop, calls=%fused_computation.122 | loop fusion | flops 7864320 | bytes 14432256 | tf_op jit(solution)/shard_map/convert_element_type | solution.py:72
  65.3 4.1 %all-to-all-start = ((bf16[128,8,384]{0,2,1:T(8,128)(2,1)}), bf16[128,8,384]{0,2,1:T(8,128)(2,1)S(1)}, u32[]{:S(2)}, u32[]{:S(2)}) async-start(bf16[128,8,384]{0,2,1:T(8,128)(2,1)} %bitcast.16), calls=%async_computation | async-start | bytes 1572864 | tf_op jit(solution)/shard_map/all_to_all | solution.py:73
  69.4 19.6 %multiply_convert_fusion = bf16[2048,1024]{1,0:T(8,128)(2,1)} fusion(f32[2048]{0:T(1024)S(1)} %bitcast.59, f32[2048]{0:T(1024)S(1)} %bitcast.52, f32[2048]{0:T(1024)S(1)} %bitcast.58, f32[2048]{0:T(1024)S(1)} %bitcast.46, f32[2048]{0:T(1024)S(1)} %bitcast.57, f32[2048]{0:T(1024)S(1)} %bitcast.47, f32[2048]{0:T(1024)S(1)} %bitcast.56, f32[2048]{0:T(1024)S(1)} %bitcast.48, ...), kind=kLoop, calls=%fused_computation | loop fusion | flops 50331648 | bytes 4341760 | tf_op jit(solution)/shard_map/convert_element_type | solution.py:66
  89.1 0.4 copy.24
  89.5 9.3 %fusion.58 = f32[1024,384]{1,0:T(8,128)} fusion(bf16[2048,1024]{1,0:T(8,128)(2,1)} %multiply_convert_fusion, f32[384]{0:T(512)S(1)} %dynamic-slice_multiply_fusion, bf16[1024,384]{1,0:T(8,128)(2,1)S(1)} %bitcast.44), kind=kOutput, calls=%fused_computation.89 | convolution fusion | flops 3227123712 | bytes 6555136 | tf_op jit(solution)/shard_map/dot_general | solution.py:79
  98.8 1.9 copy.25
  100.7 25.4 %all_to_all.64 = f32[8,128,384]{1,2,0:T(8,128)S(1)} all-to-all(f32[8,128,384]{1,2,0:T(8,128)S(1)} %copy.25), channel_id=1, replica_groups=mesh['mode'=8,'slab'=64] {'mode'}, dimensions={0} | all-to-all | bytes 3145728 | tf_op jit(solution)/shard_map/all_to_all | solution.py:84
  126.5 0.2 fusion.94
  126.8 1.9 collective-permute-start.6
  128.7 5.1 %collective-permute-start.7 = (f32[128,1,1024]{0,2,1:T(8,128)S(1)}, f32[128,1,1024]{0,2,1:T(8,128)S(1)}, u32[]{:S(2)}, u32[]{:S(2)}) collective-permute-start(f32[128,1,1024]{0,2,1:T(8,128)S(1)} %get-tuple-element.66), channel_id=1, source_target_pairs={{0,1},{1,2},{2,3},{3,4},{4,5},{5,6},{6,7},{7,8},{8,9},{9,10},{10,1... | collective-permute-start | bytes 1572872 | tf_op jit(solution)/shard_map/ppermute | solution.py:21
  133.8 0.2 fusion.91
  134.1 10.3 %collective-permute-done.6 = f32[128,1,1024]{0,2,1:T(8,128)S(1)} collective-permute-done((f32[128,1,1024]{0,2,1:T(8,128)S(1)}, f32[128,1,1024]{0,2,1:T(8,128)S(1)}, u32[]{:S(2)}, u32[]{:S(2)}) %collective-permute-start.6) | collective-permute-done | bytes 524320 | tf_op jit(solution)/shard_map/ppermute | solution.py:22
  144.4 2.5 %fusion.23 = f32[128,3,1024]{0,2,1:T(8,128)S(1)} fusion(f32[128,3,1024]{0,2,1:T(8,128)S(1)} %add.185, f32[128,1,1024]{0,2,1:T(8,128)S(1)} %collective-permute-done.7, f32[128,1,1024]{0,2,1:T(8,128)S(1)} %collective-permute-done.6, f32[128,3,992]{0,2,1:T(8,128)S(1)} %get-tuple-element.62, f32[128,3,32]{0,2,1:T(8,128)S(1)} %get-tuple-element.64, ...), kind=kLoop, calls=%fused_computation.29 | loop fusion | flops 7471104 | bytes 13645824 | tf_op jit(solution)/shard_map/add | solution.py:53
  147.2 0.2 fusion.87
  147.4 1.9 collective-permute-start.8
  149.3 5.1 %collective-permute-start.9 = (f32[128,1,1024]{0,2,1:T(8,128)S(1)}, f32[128,1,1024]{0,2,1:T(8,128)S(1)}, u32[]{:S(2)}, u32[]{:S(2)}) collective-permute-start(f32[128,1,1024]{0,2,1:T(8,128)S(1)} %get-tuple-element.52), channel_id=1, source_target_pairs={{0,1},{1,2},{2,3},{3,4},{4,5},{5,6},{6,7},{7,8},{8,9},{9,10},{10,1... | collective-permute-start | bytes 1572872 | tf_op jit(solution)/shard_map/ppermute | solution.py:21
  154.5 0.2 fusion.84
  154.7 10.3 %collective-permute-done.8 = f32[128,1,1024]{0,2,1:T(8,128)S(1)} collective-permute-done((f32[128,1,1024]{0,2,1:T(8,128)S(1)}, f32[128,1,1024]{0,2,1:T(8,128)S(1)}, u32[]{:S(2)}, u32[]{:S(2)}) %collective-permute-start.8) | collective-permute-done | bytes 524320 | tf_op jit(solution)/shard_map/ppermute | solution.py:22
  165.0 2.5 %fusion.18 = f32[128,3,1024]{0,2,1:T(8,128)S(1)} fusion(f32[128,3,1024]{0,2,1:T(8,128)S(1)} %fusion.23, f32[128,1,1024]{0,2,1:T(8,128)S(1)} %collective-permute-done.9, f32[128,1,1024]{0,2,1:T(8,128)S(1)} %collective-permute-done.8, f32[128,3,992]{0,2,1:T(8,128)S(1)} %get-tuple-element.48, f32[128,3,32]{0,2,1:T(8,128)S(1)} %get-tuple-element.50, ...), kind=kLoop, calls=%fused_computation.22 | loop fusion | flops 7471104 | bytes 13645824 | tf_op jit(solution)/shard_map/add | solution.py:53
  168.0 1.9 collective-permute-start.10
  170.0 5.1 %collective-permute-start.11 = (f32[128,1,1024]{0,2,1:T(8,128)S(1)}, f32[128,1,1024]{0,2,1:T(8,128)S(1)}, u32[]{:S(2)}, u32[]{:S(2)}) collective-permute-start(f32[128,1,1024]{0,2,1:T(8,128)S(1)} %get-tuple-element.38), channel_id=1, source_target_pairs={{0,1},{1,2},{2,3},{3,4},{4,5},{5,6},{6,7},{7,8},{8,9},{9,10},{10,1... | collective-permute-start | bytes 1572872 | tf_op jit(solution)/shard_map/ppermute | solution.py:21
  175.1 0.2 fusion.82
  175.4 10.5 %collective-permute-done.10 = f32[128,1,1024]{0,2,1:T(8,128)S(1)} collective-permute-done((f32[128,1,1024]{0,2,1:T(8,128)S(1)}, f32[128,1,1024]{0,2,1:T(8,128)S(1)}, u32[]{:S(2)}, u32[]{:S(2)}) %collective-permute-start.10) | collective-permute-done | bytes 524320 | tf_op jit(solution)/shard_map/ppermute | solution.py:22
  185.9 2.6 %fusion.73 = (bf16[128,3,1024]{0,2,1:T(8,128)(2,1)S(1)}, f32[128,3,1024]{0,2,1:T(8,128)S(1)}) fusion(f32[128,3,1024]{0,2,1:T(8,128)S(1)} %fusion.18, f32[128,1,1024]{0,2,1:T(8,128)S(1)} %collective-permute-done.11, f32[128,1,1024]{0,2,1:T(8,128)S(1)} %collective-permute-done.10, f32[128,3,1]{0,2,1:T(1,128)S(1)} %get-tuple-element.34, ...), kind=kLoop, calls=%fused_computation.121 | loop fusion | flops 7864320 | bytes 14432256 | tf_op jit(solution)/shard_map/convert_element_type | solution.py:72
  188.5 11.4 %all_to_all.65 = bf16[128,8,384]{0,2,1:T(8,128)(2,1)S(1)} all-to-all(bf16[128,8,384]{0,2,1:T(8,128)(2,1)S(1)} %bitcast.40), channel_id=1, replica_groups=mesh['mode'=8,'slab'=64] {'mode'}, dimensions={1} | all-to-all | bytes 1572864 | tf_op jit(solution)/shard_map/all_to_all | solution.py:73
  199.8 0.4 copy.26
  200.2 9.3 %fusion.61 = f32[1024,384]{1,0:T(8,128)} fusion(bf16[2048,1024]{1,0:T(8,128)(2,1)} %multiply_convert_fusion, f32[384]{0:T(512)S(1)} %dynamic-slice_multiply_fusion, bf16[1024,384]{1,0:T(8,128)(2,1)S(1)} %bitcast.43), kind=kOutput, calls=%fused_computation.90 | convolution fusion | flops 3227123712 | bytes 6555136 | tf_op jit(solution)/shard_map/dot_general | solution.py:79
  209.5 1.9 copy.27
  211.3 20.2 %all_to_all.66 = f32[8,128,384]{1,2,0:T(8,128)S(1)} all-to-all(f32[8,128,384]{1,2,0:T(8,128)S(1)} %copy.27), channel_id=1, replica_groups=mesh['mode'=8,'slab'=64] {'mode'}, dimensions={0} | all-to-all | bytes 3145728 | tf_op jit(solution)/shard_map/all_to_all | solution.py:84
  231.8 1.6 copy.28
  (54 shorter events, 3.3 us)
Async XLA Ops:
  2.0 12.2 %collective-permute-start = (f32[128,1,1024]{0,2,1:T(8,128)S(1)}, f32[128,1,1024]{0,2,1:T(8,128)S(1)}, u32[]{:S(2)}, u32[]{:S(2)}) collective-permute-start(f32[128,1,1024]{0,2,1:T(8,128)S(1)} %get-tuple-element.107), channel_id=1, source_target_pairs={{1,0},{2,1},{3,2},{4,3},{5,4},{6,5},{7,6},{8,7},{9,8},{10,9},{11,1... | collective-permute-start | bytes 1572872 | tf_op jit(solution)/shard_map/ppermute | solution.py:22
  4.5 15.4 %collective-permute-start.1 = (f32[128,1,1024]{0,2,1:T(8,128)S(1)}, f32[128,1,1024]{0,2,1:T(8,128)S(1)}, u32[]{:S(2)}, u32[]{:S(2)}) collective-permute-start(f32[128,1,1024]{0,2,1:T(8,128)S(1)} %get-tuple-element.108), channel_id=1, source_target_pairs={{0,1},{1,2},{2,3},{3,4},{4,5},{5,6},{6,7},{7,8},{8,9},{9,10},{10,1... | collective-permute-start | bytes 1572872 | tf_op jit(solution)/shard_map/ppermute | solution.py:21
  9.8 0.8 copy-start.2
  9.8 0.9 copy-start.1
  9.8 10.2 %copy-start = (f32[3,1024]{1,0:T(4,128)S(1)}, f32[3,1024]{1,0:T(4,128)}, u32[]{:S(2)}) copy-start(f32[3,1024]{1,0:T(4,128)} %param.6) | copy-start | bytes 36868
  23.0 18.4 %collective-permute-start.2 = (f32[128,1,1024]{0,2,1:T(8,128)S(1)}, f32[128,1,1024]{0,2,1:T(8,128)S(1)}, u32[]{:S(2)}, u32[]{:S(2)}) collective-permute-start(f32[128,1,1024]{0,2,1:T(8,128)S(1)} %get-tuple-element.93), channel_id=1, source_target_pairs={{1,0},{2,1},{3,2},{4,3},{5,4},{6,5},{7,6},{8,7},{9,8},{10,9},{11,1... | collective-permute-start | bytes 1572872 | tf_op jit(solution)/shard_map/ppermute | solution.py:22
  25.8 15.6 %collective-permute-start.3 = (f32[128,1,1024]{0,2,1:T(8,128)S(1)}, f32[128,1,1024]{0,2,1:T(8,128)S(1)}, u32[]{:S(2)}, u32[]{:S(2)}) collective-permute-start(f32[128,1,1024]{0,2,1:T(8,128)S(1)} %get-tuple-element.94), channel_id=1, source_target_pairs={{0,1},{1,2},{2,3},{3,4},{4,5},{5,6},{6,7},{7,8},{8,9},{9,10},{10,1... | collective-permute-start | bytes 1572872 | tf_op jit(solution)/shard_map/ppermute | solution.py:21
  44.4 17.6 %collective-permute-start.4 = (f32[128,1,1024]{0,2,1:T(8,128)S(1)}, f32[128,1,1024]{0,2,1:T(8,128)S(1)}, u32[]{:S(2)}, u32[]{:S(2)}) collective-permute-start(f32[128,1,1024]{0,2,1:T(8,128)S(1)} %get-tuple-element.79), channel_id=1, source_target_pairs={{1,0},{2,1},{3,2},{4,3},{5,4},{6,5},{7,6},{8,7},{9,8},{10,9},{11,1... | collective-permute-start | bytes 1572872 | tf_op jit(solution)/shard_map/ppermute | solution.py:22
  46.4 15.7 %collective-permute-start.5 = (f32[128,1,1024]{0,2,1:T(8,128)S(1)}, f32[128,1,1024]{0,2,1:T(8,128)S(1)}, u32[]{:S(2)}, u32[]{:S(2)}) collective-permute-start(f32[128,1,1024]{0,2,1:T(8,128)S(1)} %get-tuple-element.80), channel_id=1, source_target_pairs={{0,1},{1,2},{2,3},{3,4},{4,5},{5,6},{6,7},{7,8},{8,9},{9,10},{10,1... | collective-permute-start | bytes 1572872 | tf_op jit(solution)/shard_map/ppermute | solution.py:21
  65.3 23.8 %all-to-all-start = ((bf16[128,8,384]{0,2,1:T(8,128)(2,1)}), bf16[128,8,384]{0,2,1:T(8,128)(2,1)S(1)}, u32[]{:S(2)}, u32[]{:S(2)}) async-start(bf16[128,8,384]{0,2,1:T(8,128)(2,1)} %bitcast.16), calls=%async_computation | async-start | bytes 1572864 | tf_op jit(solution)/shard_map/all_to_all | solution.py:73
  69.4 19.6 %copy-start.3 = (f32[3,1024]{1,0:T(4,128)S(1)}, f32[3,1024]{1,0:T(4,128)}, u32[]{:S(2)}) copy-start(f32[3,1024]{1,0:T(4,128)} %param.7) | copy-start | bytes 36868
  126.8 17.6 %collective-permute-start.6 = (f32[128,1,1024]{0,2,1:T(8,128)S(1)}, f32[128,1,1024]{0,2,1:T(8,128)S(1)}, u32[]{:S(2)}, u32[]{:S(2)}) collective-permute-start(f32[128,1,1024]{0,2,1:T(8,128)S(1)} %get-tuple-element.65), channel_id=1, source_target_pairs={{1,0},{2,1},{3,2},{4,3},{5,4},{6,5},{7,6},{8,7},{9,8},{10,9},{11,1... | collective-permute-start | bytes 1572872 | tf_op jit(solution)/shard_map/ppermute | solution.py:22
  128.7 15.7 %collective-permute-start.7 = (f32[128,1,1024]{0,2,1:T(8,128)S(1)}, f32[128,1,1024]{0,2,1:T(8,128)S(1)}, u32[]{:S(2)}, u32[]{:S(2)}) collective-permute-start(f32[128,1,1024]{0,2,1:T(8,128)S(1)} %get-tuple-element.66), channel_id=1, source_target_pairs={{0,1},{1,2},{2,3},{3,4},{4,5},{5,6},{6,7},{7,8},{8,9},{9,10},{10,1... | collective-permute-start | bytes 1572872 | tf_op jit(solution)/shard_map/ppermute | solution.py:21
  147.4 17.6 %collective-permute-start.8 = (f32[128,1,1024]{0,2,1:T(8,128)S(1)}, f32[128,1,1024]{0,2,1:T(8,128)S(1)}, u32[]{:S(2)}, u32[]{:S(2)}) collective-permute-start(f32[128,1,1024]{0,2,1:T(8,128)S(1)} %get-tuple-element.51), channel_id=1, source_target_pairs={{1,0},{2,1},{3,2},{4,3},{5,4},{6,5},{7,6},{8,7},{9,8},{10,9},{11,1... | collective-permute-start | bytes 1572872 | tf_op jit(solution)/shard_map/ppermute | solution.py:22
  149.3 15.7 %collective-permute-start.9 = (f32[128,1,1024]{0,2,1:T(8,128)S(1)}, f32[128,1,1024]{0,2,1:T(8,128)S(1)}, u32[]{:S(2)}, u32[]{:S(2)}) collective-permute-start(f32[128,1,1024]{0,2,1:T(8,128)S(1)} %get-tuple-element.52), channel_id=1, source_target_pairs={{0,1},{1,2},{2,3},{3,4},{4,5},{5,6},{6,7},{7,8},{8,9},{9,10},{10,1... | collective-permute-start | bytes 1572872 | tf_op jit(solution)/shard_map/ppermute | solution.py:21
  168.0 17.8 %collective-permute-start.10 = (f32[128,1,1024]{0,2,1:T(8,128)S(1)}, f32[128,1,1024]{0,2,1:T(8,128)S(1)}, u32[]{:S(2)}, u32[]{:S(2)}) collective-permute-start(f32[128,1,1024]{0,2,1:T(8,128)S(1)} %get-tuple-element.37), channel_id=1, source_target_pairs={{1,0},{2,1},{3,2},{4,3},{5,4},{6,5},{7,6},{8,7},{9,8},{10,9},{11,1... | collective-permute-start | bytes 1572872 | tf_op jit(solution)/shard_map/ppermute | solution.py:22
  170.0 15.9 %collective-permute-start.11 = (f32[128,1,1024]{0,2,1:T(8,128)S(1)}, f32[128,1,1024]{0,2,1:T(8,128)S(1)}, u32[]{:S(2)}, u32[]{:S(2)}) collective-permute-start(f32[128,1,1024]{0,2,1:T(8,128)S(1)} %get-tuple-element.38), channel_id=1, source_target_pairs={{0,1},{1,2},{2,3},{3,4},{4,5},{5,6},{6,7},{7,8},{8,9},{9,10},{10,1... | collective-permute-start | bytes 1572872 | tf_op jit(solution)/shard_map/ppermute | solution.py:21
where the time goes:
time: 234 us; the launch traced here: 233 us
  waiting for transfers between devices  60.7 us (26%)
  blocking collectives  56.9 us (24%)
  starting transfers between devices  47.5 us (20%)
  other arithmetic  36 us (15%)
  matrix products  18.6 us (8%)
  local copies, waits for them, and re-layouts  13.1 us (6%)
    ppermute x6, waiting for transfers between devices, with_halo(): after = lax.ppermute(leading, axis, down)  54.9 us
    all_to_all x2, blocking collectives, per_device(): lax.all_to_all(increment, 'mode', split_axis=0, concat_axis=1, tiled=True)  45.6 us
    ppermute x6, starting transfers between devices, with_halo(): before = lax.ppermute(last, axis, up)  30.4 us
    convert_element_type x1, other arithmetic, per_device(): basis_low = make_basis(mode_table, point_index).astype(jnp.bfloat16)  19.6 us
    dot_general x2, matrix products, per_device(): lax.dot_general(basis_low, reaction, (((0,), (0,)), ((), ())), preferred_...  18.6 us
    ppermute x6, starting transfers between devices, with_halo(): after = lax.ppermute(leading, axis, down)  13 us
    all_to_all x1, blocking collectives, per_device(): lax.all_to_all(flat_low, 'mode', split_axis=1, concat_axis=0, tiled=True)  11.4 us
    add x4, other arithmetic, sweep(): return middle + kappa_mid[None] * (beside_all - 6.0 * middle)  9.87 us
  transfers between devices with their start and end apart: 13, of which 7 were waited for; matrix products, arithmetic and copies ran while one was open for 9% of the time, Pallas kernels for 0%

commit v1 on v0

v1 whole, which is shorter than its diff:
```python
import functools
import jax
import jax.numpy as jnp
from jax import lax
from jax.experimental import pallas as pl
from jax.experimental.pallas import tpu as pltpu
from jax.sharding import PartitionSpec as P

MESH = pl.DeviceIdType.MESH
F32, BF16, I16, I32 = jnp.float32, jnp.bfloat16, jnp.int16, jnp.int32
MODES = 1024
POINTS = 2048
SWEEPS = 3
L = 128
GROUPS = MODES // L
ROWS = 384
HALF = ROWS // 2
NCH = 4
GPC = GROUPS // NCH
FACES = (48, 48, 48, 48, 64, 64)
OFFS = (0, 48, 96, 144, 192, 256)
FROWS = 320
STEP = 32000.0
INV_LN2 = 1.4426950408889634


def kernel(
    x_hbm, dif_hbm, gro_hbm, mt_hbm, pi_hbm, out_hbm,
    xs, kg_src, mt, pi, tr, snd, rcv, kg_rcv, kap, gro, cellmap,
    fld, fsnd, frcv, basis, low, react, fin, fin_rcv,
    in_sem, a_send, a_recv, kg_send, kg_recv, h_send, h_recv, f_send, f_recv, out_sem,
):
    m, s = lax.axis_index("mode"), lax.axis_index("slab")
    depth = lax.axis_size("slab") // 4
    cx, ylo = m % 4, m // 4
    core, yhi, cz = s % 2, (s // 2) % 2, s // 4
    cy = yhi * 2 + ylo

    def at(x, y, z, c):
        return ((y % 2) * 4 + x, z * 4 + (y // 2) * 2 + c)

    loads = [pltpu.make_async_copy(x_hbm.at[p], xs.at[p], in_sem.at[p]) for p in range(3)]
    loads.append(pltpu.make_async_copy(dif_hbm, kg_src.at[0], in_sem.at[3]))
    loads.append(pltpu.make_async_copy(gro_hbm, kg_src.at[1], in_sem.at[4]))
    loads.append(pltpu.make_async_copy(mt_hbm, mt, in_sem.at[5]))
    loads.append(pltpu.make_async_copy(pi_hbm, pi, in_sem.at[6]))
    for c in loads:
        c.start()

    zup_z = jnp.where(core == 1, (cz + 1) % depth, cz)
    zdn_z = jnp.where(core == 0, (cz + depth - 1) % depth, cz)
    up = at(cx, cy, zup_z, 1 - core)
    down = at(cx, cy, zdn_z, 1 - core)
    partners = (
        at((cx + 1) % 4, cy, cz, core),
        at((cx + 3) % 4, cy, cz, core),
        at(cx, (cy + 1) % 4, cz, core),
        at(cx, (cy + 3) % 4, cz, core),
        up,
        down,
    )

    barrier = pltpu.get_barrier_semaphore()
    place = (cy * 4 + cx) * 2 + core

    def greet(k, carry):
        q = (place + k) % 32
        pl.semaphore_signal(
            barrier, inc=1, device_id=at((q // 2) % 4, q // 8, cz, q % 2), device_id_type=MESH
        )
        return carry

    lax.fori_loop(1, 32, greet, 0)
    far_z = jnp.where(core == 1, zup_z, zdn_z)
    pl.semaphore_signal(
        barrier, inc=1, device_id=at(cx, cy, far_z, 1 - core), device_id_type=MESH
    )

    big = jnp.zeros((8, L), F32)
    for p in range(3):
        loads[p].wait()

        def turn(b, big, p=p):
            block = jnp.transpose(xs[p, :, pl.ds(pl.multiple_of(b * L, L), L)])
            tr[pl.ds(pl.multiple_of((p * 8 + b) * L, L), L), :] = block
            for i in range(16):
                big = jnp.maximum(big, jnp.abs(block[8 * i : 8 * i + 8]))
            return big

        big = lax.fori_loop(0, 8, turn, big)
    top = jnp.maximum(jnp.max(big, axis=0, keepdims=True), 1e-30)
    level = jnp.ceil(jnp.log(top) * INV_LN2)
    gain = jnp.exp2(-level) * STEP

    tag = jnp.broadcast_to(level, (16, L)).astype(I32).astype(I16)
    for d in range(16):
        snd[d, HALF : HALF + 16, :] = tag

    def code(i, carry):
        p, b = i // 8, i % 8
        for y in range(4):
            parts = [
                tr[pl.ds(pl.multiple_of(i * L + xi * 32 + y * 8, 8), 8), :] for xi in range(4)
            ]
            tile = jnp.round(jnp.concatenate(parts, axis=0) * gain).astype(I32).astype(I16)
            row = pl.multiple_of(p * 64 + (b % 2) * 32, 32)
            snd[y * 4 + b // 2, pl.ds(row, 32), :] = tile
        return carry

    lax.fori_loop(0, 24, code, 0)

    pl.semaphore_wait(barrier, 32)

    def spread(k, wait):
        px, py = (cx + k) % 4, (cy + k // 4) % 4
        return pltpu.make_async_remote_copy(
            src_ref=snd.at[py * 4 + px],
            dst_ref=rcv.at[m * 2 + core],
            send_sem=a_send.at[k],
            recv_sem=a_recv.at[m * 2 + core],
            device_id=at(px, py, cz, yhi),
            device_id_type=MESH,
        )

    own = pltpu.make_async_copy(snd.at[cy * 4 + cx], rcv.at[m * 2 + core], a_recv.at[m * 2 + core])

    @pl.when(core == yhi)
    def _():
        own.start()

    @pl.when(core != yhi)
    def _():
        spread(0, None).start()

    def spread_start(k, carry):
        spread(k, None).start()
        return carry

    lax.fori_loop(1, 16, spread_start, 0)

    loads[3].wait()
    loads[4].wait()

    def coeff(h):
        return pltpu.make_async_remote_copy(
            src_ref=kg_src,
            dst_ref=kg_rcv.at[core],
            send_sem=kg_send.at[h],
            recv_sem=kg_recv.at[core],
            device_id=(m, cz * 4 + h * 2 + yhi),
            device_id_type=MESH,
        )

    kg_own = pltpu.make_async_copy(kg_src, kg_rcv.at[core], kg_recv.at[core])

    @pl.when(core == yhi)
    def _():
        kg_own.start()
        coeff(1 - yhi).start()

    @pl.when(core != yhi)
    def _():
        coeff(yhi).start()
        coeff(1 - yhi).start()

    loads[5].wait()
    loads[6].wait()
    k8 = lax.broadcasted_iota(I32, (8, 8), 1)
    r8 = lax.broadcasted_iota(I32, (8, 8), 0)
    power = jnp.where(
        k8 % 4 == 0, 1.0, jnp.where(k8 % 4 == 1, 3.0, jnp.where(k8 % 4 == 2, 9.0, 27.0))
    )
    weight = jnp.where(k8 // 4 == r8, power, 0.0).astype(BF16)
    codes = lax.dot_general(
        weight, mt[...].astype(F32).astype(BF16), (((1,), (1,)), ((), ())),
        preferred_element_type=F32,
    )
    hot_row = lax.broadcasted_iota(I32, (256, MODES), 0)
    hot_key = jnp.where(hot_row < 243, hot_row % 81, -1).astype(F32)
    hots = [
        jnp.where(hot_key == codes[j : j + 1, :], 1.0, 0.0).astype(BF16) for j in range(2)
    ]
    lane = lax.broadcasted_iota(I32, (8, 256), 1)
    combo = lane % 81
    digits = [(combo // 3**j) % 3 for j in range(4)]
    third = lane // 81
    QB = 64

    def build(i, carry):
        base = pl.multiple_of(i * QB, QB)
        picked = []
        for j in range(2):
            tiles = []
            for t in range(QB // 8):
                node = pi[pl.ds(base + t * 8, 8), :].astype(F32)
                first = (node - 3.0) * 0.32
                result = None
                for d in range(4):
                    h1 = jnp.broadcast_to(first[:, j * 4 + d : j * 4 + d + 1], (8, 256))
                    h2 = (h1 * h1 - 1.0) * 0.7071067811865476
                    factor = jnp.where(digits[d] == 0, 1.0, jnp.where(digits[d] == 1, h1, h2))
                    result = factor if result is None else result * factor
                high = result.astype(BF16).astype(F32)
                rest = result - high
                mid = rest.astype(BF16).astype(F32)
                tail = rest - mid
                tiles.append(jnp.where(third == 0, high, jnp.where(third == 1, mid, tail)))
            table = jnp.concatenate(tiles, axis=0).astype(BF16)
            picked.append(jnp.dot(table, hots[j], preferred_element_type=F32))
        basis[pl.ds(base, QB), :] = (picked[0] * picked[1]).astype(BF16)
        return carry

    lax.fori_loop(0, POINTS // QB, build, 0)

    for c in range(2):
        pltpu.make_async_copy(kg_rcv.at[c], kg_rcv.at[c], kg_recv.at[c]).wait()
    for c in range(2):
        for b in range(2):
            cols = pl.ds(pl.multiple_of(cx * 256 + b * L, L), L)
            rows8 = [kg_rcv[c, 0, :, cols], kg_rcv[c, 1, :, cols], jnp.zeros((L - 6, L), F32)]
            cellmap[...] = jnp.transpose(jnp.concatenate(rows8, axis=0))
            for xi in range(4):
                tile = cellmap[pl.ds(pl.multiple_of(xi * 32 + cy * 8, 8), 8), :]
                for p in range(3):
                    to = (c * 3 + p) * 64 + (b * 4 + xi) * 8
                    kap[to : to + 8, :] = jnp.broadcast_to(tile[:, p : p + 1], (8, L))
                    gro[to : to + 8, :] = jnp.broadcast_to(tile[:, 3 + p : 4 + p], (8, L)) * 0.125

    def face_copies(sw, ch):
        out = []
        for f in range(6):
            rows = pl.ds(OFFS[f] * GPC, FACES[f] * GPC)
            out.append(
                pltpu.make_async_remote_copy(
                    src_ref=fsnd.at[sw, ch, rows],
                    dst_ref=frcv.at[sw, ch, rows],
                    send_sem=h_send.at[sw],
                    recv_sem=h_recv.at[sw, ch],
                    device_id=partners[f],
                    device_id_type=MESH,
                )
            )
        return out

    def send_faces(sw, par, ch):
        def fill(gg, carry):
            g = ch * GPC + gg

            def put(f, value):
                row = pl.multiple_of(OFFS[f] * GPC + gg * FACES[f], 16)
                fsnd[sw, ch, pl.ds(row, FACES[f]), :] = value.astype(BF16)

            put(0, jnp.concatenate([fld[par, g, z * 64 + 56 : z * 64 + 64, :] for z in range(6)], 0))
            put(1, jnp.concatenate([fld[par, g, z * 64 : z * 64 + 8, :] for z in range(6)], 0))
            put(2, jnp.concatenate([fld[par, g, pl.ds(z * 64 + 7, 8, stride=8), :] for z in range(6)], 0))
            put(3, jnp.concatenate([fld[par, g, pl.ds(z * 64, 8, stride=8), :] for z in range(6)], 0))
            put(4, fld[par, g, 320:384, :])
            put(5, fld[par, g, 0:64, :])
            return carry

        lax.fori_loop(0, GPC, fill, 0)
        for c in face_copies(sw, ch):
            c.start()

    first_plane = jnp.logical_and(cz == 0, core == 0)
    last_plane = jnp.logical_and(cz == depth - 1, core == 1)
    sub = lax.broadcasted_iota(I32, (8, L), 0)

    def sweep(sw, ch):
        par = sw % 2
        pltpu.make_async_copy(frcv.at[sw, ch], frcv.at[sw, ch], h_recv.at[sw, ch]).wait()

        def group(gg, carry):
            g = ch * GPC + gg

            def halo(f):
                row = pl.multiple_of(OFFS[f] * GPC + gg * FACES[f], 16)
                return frcv[sw, ch, pl.ds(row, FACES[f]), :].astype(F32)

            xl, xh, yl, yh = halo(0), halo(1), halo(2), halo(3)
            zl = jnp.where(first_plane, 0.0, halo(4))
            zh = jnp.where(last_plane, 0.0, halo(5))
            for z in range(6):
                for x in range(8):
                    r = z * 64 + x * 8
                    mid = fld[par, g, r : r + 8, :]
                    xm = fld[par, g, r - 8 : r, :] if x else xl[z * 8 : z * 8 + 8]
                    xp = fld[par, g, r + 8 : r + 16, :] if x < 7 else xh[z * 8 : z * 8 + 8]
                    zm = fld[par, g, r - 64 : r - 56, :] if z else zl[x * 8 : x * 8 + 8]
                    zp = fld[par, g, r + 64 : r + 72, :] if z < 5 else zh[x * 8 : x * 8 + 8]
                    e = z * 8 + x
                    ym = jnp.where(sub == 0, yl[e : e + 1], pltpu.roll(mid, 1, 0))
                    yp = jnp.where(sub == 7, yh[e : e + 1], pltpu.roll(mid, 7, 0))
                    total = ((xm + xp) + (ym + yp)) + (zp + zm)
                    fld[1 - par, g, r : r + 8, :] = mid + kap[r : r + 8, :] * (total - 6.0 * mid)
            return carry

        lax.fori_loop(0, GPC, group, 0)

    def lower(par, ch):
        for gg in range(GPC):
            col = pl.ds(pl.multiple_of((ch * GPC + gg) * L, L), L)
            low[:, col] = fld[par, ch * GPC + gg].astype(BF16)

    def diffuse(first_sweep):
        def one(i, carry):
            t, ch = i // NCH, i % NCH
            sw = first_sweep + t
            sweep(sw, ch)

            @pl.when(t < SWEEPS - 1)
            def _():
                send_faces(sw + 1, (sw + 1) % 2, ch)

            @pl.when(t == SWEEPS - 1)
            def _():
                lower((sw + 1) % 2, ch)

            return carry

        lax.fori_loop(0, SWEEPS * NCH, one, 0)

    QC = 256

    def forward(i, carry):
        at_q = pl.ds(pl.multiple_of(i * QC, QC), QC)
        v = lax.dot_general(
            low[...], basis[at_q, :], (((1,), (1,)), ((), ())), preferred_element_type=F32
        )
        rate = jnp.concatenate([gro[...]] * (QC // L), axis=1)
        react[:, at_q] = (v * (rate - (v * v) * (1.0 / 128.0))).astype(BF16)
        return carry

    def increment(ch):
        cols = pl.ds(pl.multiple_of(ch * GPC * L, GPC * L), GPC * L)
        inc = jnp.dot(react[...], basis[:, cols], preferred_element_type=F32)
        return inc * (1.4 * MODES**0.5 / POINTS)

    def arrive(ch, carry):
        def one(gg, carry):
            g = ch * GPC + gg
            for c in range(2):
                slot = g * 2 + c
                pltpu.make_async_copy(rcv.at[slot], rcv.at[slot], a_recv.at[slot]).wait()
                level = rcv[slot, HALF : HALF + 16, :].astype(I32).astype(F32)[0:1]
                unit = jnp.exp2(level) * (1.0 / STEP)
                fld[0, g, c * HALF : (c + 1) * HALF, :] = (
                    rcv[slot, 0:HALF, :].astype(I32).astype(F32) * unit
                )
            return carry

        lax.fori_loop(0, GPC, one, 0)
        send_faces(0, 0, ch)
        return carry

    lax.fori_loop(0, NCH, arrive, 0)

    diffuse(0)
    lax.fori_loop(0, POINTS // QC, forward, 0)

    def back(ch, carry):
        inc = increment(ch)
        for gg in range(GPC):
            fld[1, ch * GPC + gg] += inc[:, gg * L : (gg + 1) * L]
        send_faces(SWEEPS, 1, ch)
        return carry

    lax.fori_loop(0, NCH, back, 0)
    diffuse(SWEEPS)
    lax.fori_loop(0, POINTS // QC, forward, 0)

    patch = cy * 4 + cx

    def home(g, c):
        return pltpu.make_async_remote_copy(
            src_ref=fin.at[g * 2 + c],
            dst_ref=fin_rcv.at[patch],
            send_sem=f_send.at[g * 2 + c],
            recv_sem=f_recv.at[patch],
            device_id=(g, cz * 4 + core * 2 + c),
            device_id_type=MESH,
        )

    def stays(g, c):
        return pltpu.make_async_copy(fin.at[g * 2 + c], fin_rcv.at[patch], f_recv.at[patch])

    def is_own(g, c):
        return jnp.logical_and(g == m, jnp.logical_and(core == yhi, c == core))

    def finish(ch, carry):
        inc = increment(ch)
        for gg in range(GPC):
            g = ch * GPC + gg
            done = (fld[0, g] + inc[:, gg * L : (gg + 1) * L]).astype(BF16)
            for c in range(2):
                fin[g * 2 + c] = done[c * HALF : (c + 1) * HALF]

                @pl.when(is_own(g, c))
                def _():
                    stays(g, c).start()

                @pl.when(jnp.logical_not(is_own(g, c)))
                def _():
                    home(g, c).start()

        return carry

    lax.fori_loop(0, NCH, finish, 0)

    def collect(i, carry):
        pltpu.make_async_copy(fin_rcv.at[i], fin_rcv.at[i], f_recv.at[i]).wait()
        return carry

    lax.fori_loop(0, 16, collect, 0)
    stores = [pltpu.make_async_copy(xs.at[p], out_hbm.at[p], out_sem.at[p]) for p in range(3)]
    for p in range(3):

        def unturn(b, carry, p=p):
            row = pl.multiple_of(p * 64 + (b % 2) * 32, 32)
            patches = [
                fin_rcv[y * 4 + b // 2, pl.ds(row, 32), :].astype(F32) for y in range(4)
            ]
            block = jnp.concatenate(
                [patches[y][xi * 8 : xi * 8 + 8] for xi in range(4) for y in range(4)], axis=0
            )
            xs[p, :, pl.ds(pl.multiple_of(b * L, L), L)] = jnp.transpose(block)
            return carry

        lax.fori_loop(0, 8, unturn, 0)
        stores[p].start()

    @pl.when(core != yhi)
    def _():
        spread(0, None).wait_send()
        coeff(yhi).wait_send()
        coeff(1 - yhi).wait_send()

    @pl.when(core == yhi)
    def _():
        coeff(1 - yhi).wait_send()

    def spread_done(k, carry):
        spread(k, None).wait_send()
        return carry

    lax.fori_loop(1, 16, spread_done, 0)

    def faces_done(sw, carry):
        pltpu.make_async_copy(fsnd.at[sw], fsnd.at[sw], h_send.at[sw]).wait()
        return carry

    lax.fori_loop(0, 2 * SWEEPS, faces_done, 0)

    def home_done(i, carry):
        g, c = i // 2, i % 2

        @pl.when(jnp.logical_not(is_own(g, c)))
        def _():
            home(g, c).wait_send()

        return carry

    lax.fori_loop(0, 16, home_done, 0)
    for p in range(3):
        stores[p].wait()


def per_device(chaos_field, diffusivity, growth_rate, mode_table, point_index):
    any_spec = pl.BlockSpec(memory_space=pl.ANY)
    V = pltpu.VMEM
    DMA = pltpu.SemaphoreType.DMA
    planes_first = jnp.transpose(chaos_field, (1, 0, 2))
    result = pl.pallas_call(
        kernel,
        out_shape=jax.ShapeDtypeStruct(planes_first.shape, F32),
        in_specs=[any_spec] * 5,
        out_specs=any_spec,
        scratch_shapes=[
            V((3, L, 1024), F32),
            V((2, 3, 1024), F32),
            V((MODES, 8), I32),
            V((POINTS, 8), I32),
            V((3 * 1024, L), F32),
            V((16, HALF + 16, L), I16),
            V((16, HALF + 16, L), I16),
            V((2, 2, 3, 1024), F32),
            V((ROWS, L), F32),
            V((ROWS, L), F32),
            V((L, L), F32),
            V((2, GROUPS, ROWS, L), F32),
            V((2 * SWEEPS, NCH, FROWS * GPC, L), BF16),
            V((2 * SWEEPS, NCH, FROWS * GPC, L), BF16),
            V((POINTS, MODES), BF16),
            V((ROWS, MODES), BF16),
            V((ROWS, POINTS), BF16),
            V((16, HALF, L), BF16),
            V((16, HALF, L), BF16),
            DMA((7,)),
            DMA((16,)),
            DMA((16,)),
            DMA((2,)),
            DMA((2,)),
            DMA((2 * SWEEPS,)),
            DMA((2 * SWEEPS, NCH)),
            DMA((16,)),
            DMA((16,)),
            DMA((3,)),
        ],
        compiler_params=pltpu.CompilerParams(
            collective_id=0, has_side_effects=True, vmem_limit_bytes=52 * 1024 * 1024
        ),
    )(planes_first, diffusivity, growth_rate, mode_table, point_index)
    return jnp.transpose(result, (1, 0, 2))


def solution(mesh):
    return jax.shard_map(
        per_device,
        mesh=mesh,
        in_specs=(P("mode", "slab", None), P("slab", None), P("slab", None), P(), P()),
        out_specs=P("mode", "slab", None),
        check_vma=False,
    )
```

time: 234 us -> 91.1 us (0.39)
  the two profiles are of different devices: /device:TPU:129 before, /device:TPU:1 now
where the time goes in v1:
time: 91.1 us; the launch traced here: 90.8 us
  Pallas kernels  85.9 us (94%)
  local copies, waits for them, and re-layouts  4.87 us (5%)
    pallas_call x1, Pallas kernels, per_device(): pl.pallas_call(kernel, out_shape=jax.ShapeDtypeStruct(planes_first.shape,...  85.9 us
    unnamed x7, local copies, waits for them, and re-layouts  4.87 us

profile of v1, /device:TPU:1, one launch (start us, length us, event | category | flops | bytes accessed | tf_op | source)
XLA Modules:
  0.0 90.8 jit_solution(5856778796383529839)
XLA Ops:
  0.0 0.0 copy-start.1
  0.0 0.0 copy-start
  0.0 1.0 %copy.6.mt_hbm = s32[1024,8]{1,0:T(8,128)S(1)} copy(s32[1024,8]{0,1:T(8,128)} %param.8) | data formatting | bytes 65536 | tf_op args[3]
  1.0 1.2 %copy.7.pi_hbm = s32[2048,8]{1,0:T(8,128)S(1)} copy(s32[2048,8]{0,1:T(8,128)} %param.9) | data formatting | bytes 131072 | tf_op args[4]
  2.2 0.0 copy-done.1
  2.2 0.0 copy-done
  2.2 85.9 %shard_map.55 = f32[3,128,1024]{2,1,0:T(8,128)} custom-call(f32[3,128,1024]{2,1,0:T(8,128)} %bitcast.3, f32[3,1024]{1,0:T(4,128)S(1)} %copy-done, f32[3,1024]{1,0:T(4,128)S(1)} %copy-done.1, s32[1024,8]{1,0:T(8,128)S(1)} %copy.6.mt_hbm, s32[2048,8]{1,0:T(8,128)S(1)} %copy.7.pi_hbm), custom_call_target="tpu_custom_call" | custom-call | tf_op jit(solution)/shard_map/pallas_call | solution.py:473
  88.1 2.7 %copy.9 = f32[128,3,1024]{2,0,1:T(8,128)} copy(f32[128,3,1024]{2,0,1:T(8,128)} %bitcast.2) | data formatting | bytes 3145728
Async XLA Ops:
  0.0 2.2 %copy-start.1 = (f32[3,1024]{1,0:T(4,128)S(1)}, f32[3,1024]{1,0:T(4,128)}, u32[]{:S(2)}) copy-start(f32[3,1024]{1,0:T(4,128)} %gro_hbm.1) | copy-start | bytes 36868
  0.0 2.2 %copy-start = (f32[3,1024]{1,0:T(4,128)S(1)}, f32[3,1024]{1,0:T(4,128)}, u32[]{:S(2)}) copy-start(f32[3,1024]{1,0:T(4,128)} %dif_hbm.1) | copy-start | bytes 36868

commit v2 on v1

v2 whole, which is shorter than its diff:
```python
import functools
import jax
import jax.numpy as jnp
from jax import lax
from jax.experimental import pallas as pl
from jax.experimental.pallas import tpu as pltpu
from jax.sharding import PartitionSpec as P

MESH = pl.DeviceIdType.MESH
F32, BF16, I16, I32 = jnp.float32, jnp.bfloat16, jnp.int16, jnp.int32
MODES = 1024
POINTS = 2048
SWEEPS = 3
L = 128
GROUPS = MODES // L
ROWS = 384
HALF = ROWS // 2
NCH = 4
GPC = GROUPS // NCH
FACES = (48, 48, 48, 48, 64, 64)
OFFS = (0, 48, 96, 144, 192, 256)
FROWS = 320
COMBOS = 96
STEP = 32000.0
INV_LN2 = 1.4426950408889634


def kernel(
    x_hbm, dif_hbm, gro_hbm, mt_hbm, pi_hbm, out_hbm,
    xs, kg_src, mt, pi, hot, digit, tab, gain, snd, rcv, kg_rcv, kap, gro, cellmap,
    fld0, fld1, edge, nothing, fsnd, frcv, basis, low, react, fin, fin_rcv, done_low,
    in_sem, a_send, a_recv, kg_send, kg_recv, h_send, h_recv, f_send, f_recv, out_sem,
):
    m, s = lax.axis_index("mode"), lax.axis_index("slab")
    depth = lax.axis_size("slab") // 4
    cx, ylo = m % 4, m // 4
    core, yhi, cz = s % 2, (s // 2) % 2, s // 4
    cy = yhi * 2 + ylo

    def at(x, y, z, c):
        return ((y % 2) * 4 + x, z * 4 + (y // 2) * 2 + c)

    loads = [pltpu.make_async_copy(x_hbm.at[p], xs.at[p], in_sem.at[p]) for p in range(3)]
    loads.append(pltpu.make_async_copy(dif_hbm, kg_src.at[0], in_sem.at[3]))
    loads.append(pltpu.make_async_copy(gro_hbm, kg_src.at[1], in_sem.at[4]))
    loads.append(pltpu.make_async_copy(mt_hbm, mt, in_sem.at[5]))
    loads.append(pltpu.make_async_copy(pi_hbm, pi, in_sem.at[6]))
    for c in loads:
        c.start()

    first_plane = jnp.logical_and(cz == 0, core == 0)
    last_plane = jnp.logical_and(cz == depth - 1, core == 1)
    up = at(cx, cy, jnp.minimum(cz + core, depth - 1), 1 - core)
    down = at(cx, cy, jnp.maximum(cz + core - 1, 0), 1 - core)
    partners = (
        at((cx + 1) % 4, cy, cz, core),
        at((cx + 3) % 4, cy, cz, core),
        at(cx, (cy + 1) % 4, cz, core),
        at(cx, (cy + 3) % 4, cz, core),
        up,
        down,
    )

    barrier = pltpu.get_barrier_semaphore()
    place = (cy * 4 + cx) * 2 + core

    def greet(k, carry):
        q = (place + k) % 32
        pl.semaphore_signal(
            barrier, inc=1, device_id=at((q // 2) % 4, q // 8, cz, q % 2), device_id_type=MESH
        )
        return carry

    lax.fori_loop(1, 32, greet, 0)

    @pl.when(jnp.logical_and(core == 1, cz < depth - 1))
    def _():
        pl.semaphore_signal(barrier, inc=1, device_id=up, device_id_type=MESH)

    @pl.when(jnp.logical_and(core == 0, cz > 0))
    def _():
        pl.semaphore_signal(barrier, inc=1, device_id=down, device_id_type=MESH)

    nothing[...] = jnp.zeros_like(nothing)

    for p in range(3):
        loads[p].wait()
    big = jnp.zeros((L, L), F32)
    for p in range(3):
        for b in range(8):
            big = jnp.maximum(big, jnp.abs(xs[p, :, b * L : (b + 1) * L]))
    top = jnp.broadcast_to(jnp.max(big, axis=1, keepdims=True), (L, L))
    level = jnp.ceil(jnp.log(jnp.maximum(top, 1e-30)) * INV_LN2)
    gain[...] = jnp.exp2(-level) * STEP
    tag = jnp.transpose(level)[0:16].astype(I32).astype(I16)
    for d in range(16):
        snd[d, HALF : HALF + 16, :] = tag

    pl.semaphore_wait(
        barrier, 32 - jnp.logical_or(first_plane, last_plane).astype(I32)
    )

    def spread(j, i):
        px, py = (cx + j) % 4, (cy + i) % 4
        return pltpu.make_async_remote_copy(
            src_ref=snd.at[py * 4 + px],
            dst_ref=rcv.at[m * 2 + core],
            send_sem=a_send.at[j * 4 + i],
            recv_sem=a_recv.at[m * 2 + core],
            device_id=at(px, py, cz, yhi),
            device_id_type=MESH,
        )

    own = pltpu.make_async_copy(snd.at[cy * 4 + cx], rcv.at[m * 2 + core], a_recv.at[m * 2 + core])

    def spread_column(j, carry):
        px = (cx + j) % 4
        for p in range(3):
            for b in range(2):
                cols = pl.ds(pl.multiple_of(px * 256 + b * L, L), L)
                block = jnp.transpose(jnp.round(xs[p, :, cols] * gain[...]))
                for y in range(4):
                    tile = jnp.concatenate(
                        [block[xi * 32 + y * 8 : xi * 32 + y * 8 + 8] for xi in range(4)], axis=0
                    )
                    row = p * 64 + b * 32
                    snd[y * 4 + px, row : row + 32, :] = tile.astype(I32).astype(I16)
        for i in range(4):
            if i:
                spread(j, i).start()
            else:
                stay = jnp.logical_and(j == 0, core == yhi)

                @pl.when(stay)
                def _():
                    own.start()

                @pl.when(jnp.logical_not(stay))
                def _():
                    spread(j, 0).start()

        return carry

    lax.fori_loop(0, 4, spread_column, 0)

    loads[3].wait()
    loads[4].wait()

    def coeff(h):
        return pltpu.make_async_remote_copy(
            src_ref=kg_src,
            dst_ref=kg_rcv.at[core],
            send_sem=kg_send.at[h],
            recv_sem=kg_recv.at[core],
            device_id=(m, cz * 4 + h * 2 + yhi),
            device_id_type=MESH,
        )

    kg_own = pltpu.make_async_copy(kg_src, kg_rcv.at[core], kg_recv.at[core])

    @pl.when(core == yhi)
    def _():
        kg_own.start()
        coeff(1 - yhi).start()

    @pl.when(core != yhi)
    def _():
        coeff(yhi).start()
        coeff(1 - yhi).start()

    loads[5].wait()
    loads[6].wait()
    k8 = lax.broadcasted_iota(I32, (8, L), 0)
    power = jnp.where(
        k8 % 4 == 0, 1.0, jnp.where(k8 % 4 == 1, 3.0, jnp.where(k8 % 4 == 2, 9.0, 27.0))
    )
    degrees = mt[...].astype(F32).astype(BF16)
    pick_lane = lax.broadcasted_iota(I32, (MODES, L), 1)
    for j in range(2):
        weight = jnp.where(k8 // 4 == j, power, 0.0).astype(BF16)
        code_j = lax.dot_general(
            degrees, weight, (((0,), (0,)), ((), ())), preferred_element_type=F32
        ).astype(I32)
        for h in range(2):
            lane = pick_lane + h * L
            key = jnp.where(lane >= COMBOS, lane - COMBOS, lane)
            hot[j, :, h * L : (h + 1) * L] = jnp.where(key == code_j, 1.0, 0.0).astype(BF16)
    combo = lax.broadcasted_iota(I32, (COMBOS, 256), 0)
    for d in range(4):
        digit[d] = (combo // 3**d) % 3
        tab[:, 2 * COMBOS : 256, :] = jnp.zeros((2, 256 - 2 * COMBOS, 256), BF16)
    QB = 256

    def build(i, carry):
        cols = pl.ds(pl.multiple_of(i * QB, QB), QB)
        first = (pi[:, cols].astype(F32) - 3.0) * 0.32
        second = (first * first - 1.0) * 0.7071067811865476
        picked = []
        for j in range(2):
            for t in range(COMBOS // 16):
                halves = []
                for u in range(2):
                    r = t * 16 + u * 8
                    result = None
                    for d in range(4):
                        h1 = jnp.broadcast_to(first[j * 4 + d : j * 4 + d + 1], (8, QB))
                        h2 = jnp.broadcast_to(second[j * 4 + d : j * 4 + d + 1], (8, QB))
                        which = digit[d, r : r + 8, :]
                        factor = jnp.where(which == 0, 1.0, jnp.where(which == 1, h1, h2))
                        result = factor if result is None else result * factor
                    halves.append(result)
                both = jnp.concatenate(halves, axis=0)
                high = both.astype(BF16)
                tab[j, t * 16 : t * 16 + 16, :] = high
                tab[j, COMBOS + t * 16 : COMBOS + t * 16 + 16, :] = (
                    both - high.astype(F32)
                ).astype(BF16)
        for half in range(MODES // 256):
            rows = slice(half * 256, half * 256 + 256)
            picked = [
                jnp.dot(hot[j, rows, :], tab[j], preferred_element_type=F32) for j in range(2)
            ]
            basis[rows, cols] = (picked[0] * picked[1]).astype(BF16)
        return carry

    lax.fori_loop(0, POINTS // QB, build, 0)

    for c in range(2):
        pltpu.make_async_copy(kg_rcv.at[c], kg_rcv.at[c], kg_recv.at[c]).wait()
    for c in range(2):
        for b in range(2):
            cols = pl.ds(pl.multiple_of(cx * 256 + b * L, L), L)
            rows8 = [kg_rcv[c, 0, :, cols], kg_rcv[c, 1, :, cols], jnp.zeros((L - 6, L), F32)]
            cellmap[...] = jnp.transpose(jnp.concatenate(rows8, axis=0))
            for xi in range(4):
                tile = cellmap[pl.ds(pl.multiple_of(xi * 32 + cy * 8, 8), 8), :]
                for p in range(3):
                    to = (c * 3 + p) * 64 + (b * 4 + xi) * 8
                    kap[to : to + 8, :] = jnp.broadcast_to(tile[:, p : p + 1], (8, L))
                    gro[to : to + 8, :] = jnp.broadcast_to(tile[:, 3 + p : 4 + p], (8, L)) * 0.125

    def face_copy(sw, ch, f):
        rows = pl.ds(OFFS[f] * GPC, FACES[f] * GPC)
        return pltpu.make_async_remote_copy(
            src_ref=fsnd.at[sw, ch, rows],
            dst_ref=frcv.at[sw, ch, rows],
            send_sem=h_send.at[sw, max(f - 3, 0)],
            recv_sem=h_recv.at[sw, ch],
            device_id=partners[f],
            device_id_type=MESH,
        )

    def end_copy(sw, ch, f):
        rows = pl.ds(OFFS[f] * GPC, FACES[f] * GPC)
        return pltpu.make_async_copy(nothing, frcv.at[sw, ch, rows], h_recv.at[sw, ch])

    def send_faces(sw, fld, ch):
        for gg in range(GPC):
            g = ch * GPC + gg

            def put(f, value):
                row = OFFS[f] * GPC + gg * FACES[f]
                fsnd[sw, ch, row : row + FACES[f], :] = value.astype(BF16)

            put(0, jnp.concatenate([fld[g, z * 64 + 56 : z * 64 + 64, :] for z in range(6)], 0))
            put(1, jnp.concatenate([fld[g, z * 64 : z * 64 + 8, :] for z in range(6)], 0))
            put(2, jnp.concatenate([fld[g, pl.ds(z * 64 + 7, 8, stride=8), :] for z in range(6)], 0))
            put(3, jnp.concatenate([fld[g, pl.ds(z * 64, 8, stride=8), :] for z in range(6)], 0))
            put(4, fld[g, 320:384, :])
            put(5, fld[g, 0:64, :])

        for f in range(4):
            face_copy(sw, ch, f).start()

        @pl.when(jnp.logical_not(last_plane))
        def _():
            face_copy(sw, ch, 4).start()

        @pl.when(last_plane)
        def _():
            end_copy(sw, ch, 5).start()

        @pl.when(jnp.logical_not(first_plane))
        def _():
            face_copy(sw, ch, 5).start()

        @pl.when(first_plane)
        def _():
            end_copy(sw, ch, 4).start()

    sub = lax.broadcasted_iota(I32, (8, L), 0)

    def sweep(sw, old, new, ch):
        pltpu.make_async_copy(frcv.at[sw, ch], frcv.at[sw, ch], h_recv.at[sw, ch]).wait()
        for gg in range(GPC):
            g = ch * GPC + gg

            def halo(f):
                row = OFFS[f] * GPC + gg * FACES[f]
                return frcv[sw, ch, row : row + FACES[f], :].astype(F32)

            xl, xh, yl, yh, zl, zh = [halo(f) for f in range(6)]
            for z in range(6):
                edge[gg, pl.ds(z * 64, 8, stride=8), :] = yl[z * 8 : z * 8 + 8]
                edge[gg, pl.ds(z * 64 + 7, 8, stride=8), :] = yh[z * 8 : z * 8 + 8]
            for z in range(6):
                for x in range(8):
                    r = z * 64 + x * 8
                    mid = old[g, r : r + 8, :]
                    xm = old[g, r - 8 : r, :] if x else xl[z * 8 : z * 8 + 8]
                    xp = old[g, r + 8 : r + 16, :] if x < 7 else xh[z * 8 : z * 8 + 8]
                    zm = old[g, r - 64 : r - 56, :] if z else zl[x * 8 : x * 8 + 8]
                    zp = old[g, r + 64 : r + 72, :] if z < 5 else zh[x * 8 : x * 8 + 8]
                    ends = edge[gg, r : r + 8, :]
                    ym = jnp.where(sub == 0, ends, pltpu.roll(mid, 1, 0))
                    yp = jnp.where(sub == 7, ends, pltpu.roll(mid, 7, 0))
                    total = ((xm + xp) + (ym + yp)) + (zp + zm)
                    new[g, r : r + 8, :] = mid + kap[r : r + 8, :] * (total - 6.0 * mid)

    def lower(fld, ch):
        for gg in range(GPC):
            col = pl.ds(pl.multiple_of((ch * GPC + gg) * L, L), L)
            low[:, col] = fld[ch * GPC + gg].astype(BF16)

    def diffuse(first_sweep, here, there):
        for t in range(SWEEPS):
            sw = first_sweep + t

            def one(ch, carry, t=t, sw=sw, here=here, there=there):
                sweep(sw, here, there, ch)
                if t < SWEEPS - 1:
                    send_faces(sw + 1, there, ch)
                else:
                    lower(there, ch)
                return carry

            lax.fori_loop(0, NCH, one, 0)
            here, there = there, here

    QC = 256

    def forward():
        for i in range(POINTS // QC):
            at_q = slice(i * QC, (i + 1) * QC)
            v = jnp.dot(low[...], basis[:, at_q], preferred_element_type=F32)
            rate = jnp.concatenate([gro[...]] * (QC // L), axis=1)
            react[:, at_q] = (v * (rate - (v * v) * (1.0 / 128.0))).astype(BF16)

    def increment(ch):
        cols = slice(ch * GPC * L, (ch + 1) * GPC * L)
        inc = lax.dot_general(
            react[...], basis[cols, :], (((1,), (1,)), ((), ())), preferred_element_type=F32
        )
        return inc * (1.4 * MODES**0.5 / POINTS)

    def arrive(ch, carry):
        def one(gg, carry):
            g = ch * GPC + gg
            for c in range(2):
                slot = g * 2 + c
                pltpu.make_async_copy(rcv.at[slot], rcv.at[slot], a_recv.at[slot]).wait()
                level = rcv[slot, HALF : HALF + 16, :].astype(I32).astype(F32)[0:1]
                unit = jnp.exp2(level) * (1.0 / STEP)
                fld0[g, c * HALF : (c + 1) * HALF, :] = (
                    rcv[slot, 0:HALF, :].astype(I32).astype(F32) * unit
                )
            return carry

        lax.fori_loop(0, GPC, one, 0)
        send_faces(0, fld0, ch)
        return carry

    lax.fori_loop(0, NCH, arrive, 0)

    diffuse(0, fld0, fld1)
    forward()
    for ch in range(NCH):
        inc = increment(ch)
        for gg in range(GPC):
            fld1[ch * GPC + gg] += inc[:, gg * L : (gg + 1) * L]
        send_faces(SWEEPS, fld1, ch)
    diffuse(SWEEPS, fld1, fld0)
    forward()

    patch = cy * 4 + cx

    def home(g, c):
        return pltpu.make_async_remote_copy(
            src_ref=fin.at[g * 2 + c],
            dst_ref=fin_rcv.at[patch],
            send_sem=f_send.at[g * 2 + c],
            recv_sem=f_recv.at[patch],
            device_id=(g, cz * 4 + core * 2 + c),
            device_id_type=MESH,
        )

    def stays(g, c):
        return pltpu.make_async_copy(fin.at[g * 2 + c], fin_rcv.at[patch], f_recv.at[patch])

    def is_own(g, c):
        return jnp.logical_and(g == m, jnp.logical_and(core == yhi, c == core))

    for ch in range(NCH):
        inc = increment(ch)
        for gg in range(GPC):
            g = ch * GPC + gg
            done = (fld0[g] + inc[:, gg * L : (gg + 1) * L]).astype(BF16)
            for c in range(2):
                fin[g * 2 + c] = done[c * HALF : (c + 1) * HALF]

                @pl.when(is_own(g, c))
                def _():
                    stays(g, c).start()

                @pl.when(jnp.logical_not(is_own(g, c)))
                def _():
                    home(g, c).start()


    def out_copy(px):
        cols = pl.ds(pl.multiple_of(px * 256, 256), 256)
        return pltpu.make_async_copy(
            done_low.at[:, :, cols], out_hbm.at[:, :, cols], out_sem.at[px]
        )

    def collect(j, carry):
        px = (cx + j + (j // 2) * (5 - 2 * j)) % 4
        for y in range(4):
            slot = y * 4 + px
            pltpu.make_async_copy(fin_rcv.at[slot], fin_rcv.at[slot], f_recv.at[slot]).wait()
        for p in range(3):
            for b in range(2):
                row = p * 64 + b * 32
                parts = [fin_rcv[y * 4 + px, row : row + 32, :].astype(F32) for y in range(4)]
                block = jnp.concatenate(
                    [parts[y][xi * 8 : xi * 8 + 8] for xi in range(4) for y in range(4)], axis=0
                )
                cols = pl.ds(pl.multiple_of(px * 256 + b * L, L), L)
                done_low[p, :, cols] = jnp.transpose(block).astype(BF16)
        out_copy(px).start()
        return carry

    lax.fori_loop(0, 4, collect, 0)

    @pl.when(core != yhi)
    def _():
        spread(0, 0).wait_send()
        coeff(yhi).wait_send()
        coeff(1 - yhi).wait_send()

    @pl.when(core == yhi)
    def _():
        coeff(1 - yhi).wait_send()

    def spread_done(k, carry):
        spread(k // 4, k % 4).wait_send()
        return carry

    lax.fori_loop(1, 16, spread_done, 0)

    def faces_done(sw, carry):
        def sent(f, lo, hi):
            part = fsnd.at[sw, :, pl.ds(lo * GPC, (hi - lo) * GPC)]
            pltpu.make_async_copy(part, part, h_send.at[sw, f]).wait()

        sent(0, 0, 192)

        @pl.when(jnp.logical_not(last_plane))
        def _():
            sent(1, 192, 256)

        @pl.when(jnp.logical_not(first_plane))
        def _():
            sent(2, 256, 320)

        return carry

    lax.fori_loop(0, 2 * SWEEPS, faces_done, 0)

    def home_done(i, carry):
        g, c = i // 2, i % 2

        @pl.when(jnp.logical_not(is_own(g, c)))
        def _():
            home(g, c).wait_send()

        return carry

    lax.fori_loop(0, 16, home_done, 0)
    for px in range(4):
        out_copy(px).wait()


def per_device(chaos_field, diffusivity, growth_rate, mode_table, point_index):
    any_spec = pl.BlockSpec(memory_space=pl.ANY)
    V = pltpu.VMEM
    DMA = pltpu.SemaphoreType.DMA
    planes_first = jnp.transpose(chaos_field, (1, 0, 2))
    result = pl.pallas_call(
        kernel,
        out_shape=jax.ShapeDtypeStruct(planes_first.shape, BF16),
        in_specs=[pl.BlockSpec(memory_space=pltpu.HBM)] * 5,
        out_specs=any_spec,
        scratch_shapes=[
            V((3, L, 1024), F32),
            V((2, 3, 1024), F32),
            V((8, MODES), I32),
            V((8, POINTS), I32),
            V((2, MODES, 256), BF16),
            V((4, COMBOS, 256), I32),
            V((2, 256, 256), BF16),
            V((L, L), F32),
            V((16, HALF + 16, L), I16),
            V((16, HALF + 16, L), I16),
            V((2, 2, 3, 1024), F32),
            V((ROWS, L), F32),
            V((ROWS, L), F32),
            V((L, L), F32),
            V((GROUPS, ROWS, L), F32),
            V((GROUPS, ROWS, L), F32),
            V((GPC, ROWS, L), F32),
            V((64 * GPC, L), BF16),
            V((2 * SWEEPS, NCH, FROWS * GPC, L), BF16),
            V((2 * SWEEPS, NCH, FROWS * GPC, L), BF16),
            V((MODES, POINTS), BF16),
            V((ROWS, MODES), BF16),
            V((ROWS, POINTS), BF16),
            V((16, HALF, L), BF16),
            V((16, HALF, L), BF16),
            V((3, L, 1024), BF16),
            DMA((7,)),
            DMA((16,)),
            DMA((16,)),
            DMA((2,)),
            DMA((2,)),
            DMA((2 * SWEEPS, 3)),
            DMA((2 * SWEEPS, NCH)),
            DMA((16,)),
            DMA((16,)),
            DMA((4,)),
        ],
        compiler_params=pltpu.CompilerParams(
            collective_id=0, has_side_effects=True, vmem_limit_bytes=52 * 1024 * 1024
        ),
    )(planes_first, diffusivity, growth_rate, mode_table.T, point_index.T)
    return jnp.transpose(result.astype(F32), (1, 0, 2))


def solution(mesh):
    return jax.shard_map(
        per_device,
        mesh=mesh,
        in_specs=(P("mode", "slab", None), P("slab", None), P("slab", None), P(), P()),
        out_specs=P("mode", "slab", None),
        check_vma=False,
    )
```

time: 91.1 us -> 75.3 us (0.83)
  the two profiles are of different devices: /device:TPU:1 before, /device:TPU:15 now
where the time goes in v2:
time: 75.3 us; the launch traced here: 74.9 us
  Pallas kernels  70.6 us (94%)
  local copies, waits for them, and re-layouts  3.03 us (4%)
  other arithmetic  1.32 us (2%)
    pallas_call x1, Pallas kernels, per_device(): pl.pallas_call(kernel, out_shape=jax.ShapeDtypeStruct(planes_first.shape,...  70.6 us
    unnamed x8, local copies, waits for them, and re-layouts  3.03 us

profile of v2, /device:TPU:15, one launch (start us, length us, event | category | flops | bytes accessed | tf_op | source)
XLA Modules:
  0.0 74.9 jit_solution(11275713952559924032)
XLA Ops:
  0.0 0.0 copy-start
  0.0 0.8 %copy-done = s32[2048,8]{0,1:T(8,128)S(1)} copy-done((s32[2048,8]{0,1:T(8,128)S(1)}, s32[2048,8]{0,1:T(8,128)}, u32[]{:S(2)}) %copy-start) | copy-done | bytes 65560
  0.8 0.0 copy-start.1
  0.8 0.8 %copy-done.1 = s32[1024,8]{0,1:T(8,128)S(1)} copy-done((s32[1024,8]{0,1:T(8,128)S(1)}, s32[1024,8]{0,1:T(8,128)}, u32[]{:S(2)}) %copy-start.1) | copy-done | bytes 32792
  1.6 0.0 copy-start.2
  1.6 0.7 copy-done.2
  2.3 0.0 copy-start.3
  2.3 0.7 copy-done.3
  3.0 70.6 %shard_map.55 = bf16[3,128,1024]{2,1,0:T(8,128)(2,1)S(1)} custom-call(f32[3,128,1024]{2,1,0:T(8,128)} %bitcast.7, f32[3,1024]{1,0:T(4,128)S(1)} %copy-done.2, f32[3,1024]{1,0:T(4,128)S(1)} %copy-done.3, s32[8,1024]{1,0:T(8,128)S(1)} %bitcast.6, s32[8,2048]{1,0:T(8,128)S(1)} %bitcast.5), custom_call_target="tpu_custom_call" | custom-call | tf_op jit(solution)/shard_map/pallas_call | solution.py:499
  73.6 1.3 %convert_bitcast_fusion = f32[128,3,1024]{2,0,1:T(8,128)} fusion(bf16[3,128,1024]{2,1,0:T(8,128)(2,1)S(1)} %shard_map.55), kind=kLoop, calls=%fused_computation | loop fusion | flops 393216 | bytes 2359296 | tf_op jit(solution)/shard_map/transpose | solution.py:546
Async XLA Ops:
  0.0 0.8 %copy-start = (s32[2048,8]{0,1:T(8,128)S(1)}, s32[2048,8]{0,1:T(8,128)}, u32[]{:S(2)}) copy-start(s32[2048,8]{0,1:T(8,128)} %param.9) | copy-start | bytes 196612
  0.8 0.8 %copy-start.1 = (s32[1024,8]{0,1:T(8,128)S(1)}, s32[1024,8]{0,1:T(8,128)}, u32[]{:S(2)}) copy-start(s32[1024,8]{0,1:T(8,128)} %param.8) | copy-start | bytes 98308
  1.6 0.7 copy-start.2
  2.3 0.7 copy-start.3

commit v3 on v2

--- a/solution.py
+++ b/solution.py
@@ -20,6 +20,7 @@
 FACES = (48, 48, 48, 48, 64, 64)
 OFFS = (0, 48, 96, 144, 192, 256)
 FROWS = 320
+FAR = (2, 1, 3, 0)
 COMBOS = 96
 STEP = 32000.0
 INV_LN2 = 1.4426950408889634
@@ -28,7 +29,7 @@
 def kernel(
     x_hbm, dif_hbm, gro_hbm, mt_hbm, pi_hbm, out_hbm,
     xs, kg_src, mt, pi, hot, digit, tab, gain, snd, rcv, kg_rcv, kap, gro, cellmap,
-    fld0, fld1, edge, nothing, fsnd, frcv, basis, low, react, fin, fin_rcv, done_low,
+    fld0, fld1, edge, nothing, fsnd, frcv, basis, values, react, fin, fin_rcv, done_low,
     in_sem, a_send, a_recv, kg_send, kg_recv, h_send, h_recv, f_send, f_recv, out_sem,
 ):
     m, s = lax.axis_index("mode"), lax.axis_index("slab")
@@ -96,10 +97,6 @@
     for d in range(16):
         snd[d, HALF : HALF + 16, :] = tag
 
-    pl.semaphore_wait(
-        barrier, 32 - jnp.logical_or(first_plane, last_plane).astype(I32)
-    )
-
     def spread(j, i):
         px, py = (cx + j) % 4, (cy + i) % 4
         return pltpu.make_async_remote_copy(
@@ -113,8 +110,8 @@
 
     own = pltpu.make_async_copy(snd.at[cy * 4 + cx], rcv.at[m * 2 + core], a_recv.at[m * 2 + core])
 
-    def spread_column(j, carry):
-        px = (cx + j) % 4
+    def code_column(n):
+        px = (cx + FAR[n]) % 4
         for p in range(3):
             for b in range(2):
                 cols = pl.ds(pl.multiple_of(px * 256 + b * L, L), L)
@@ -125,23 +122,30 @@
                     )
                     row = p * 64 + b * 32
                     snd[y * 4 + px, row : row + 32, :] = tile.astype(I32).astype(I16)
-        for i in range(4):
-            if i:
+
+    def spread_column(n):
+        j = FAR[n]
+        for i in FAR:
+            if i or j:
                 spread(j, i).start()
             else:
-                stay = jnp.logical_and(j == 0, core == yhi)
-
-                @pl.when(stay)
+
+                @pl.when(core == yhi)
                 def _():
                     own.start()
 
-                @pl.when(jnp.logical_not(stay))
+                @pl.when(core != yhi)
                 def _():
-                    spread(j, 0).start()
-
-        return carry
-
-    lax.fori_loop(0, 4, spread_column, 0)
+                    spread(0, 0).start()
+
+    code_column(0)
+    pl.semaphore_wait(
+        barrier, 32 - jnp.logical_or(first_plane, last_plane).astype(I32)
+    )
+    spread_column(0)
+    for n in range(1, 4):
+        code_column(n)
+        spread_column(n)
 
     loads[3].wait()
     loads[4].wait()
@@ -317,34 +321,36 @@
                     total = ((xm + xp) + (ym + yp)) + (zp + zm)
                     new[g, r : r + 8, :] = mid + kap[r : r + 8, :] * (total - 6.0 * mid)
 
-    def lower(fld, ch):
-        for gg in range(GPC):
-            col = pl.ds(pl.multiple_of((ch * GPC + gg) * L, L), L)
-            low[:, col] = fld[ch * GPC + gg].astype(BF16)
+    QC = 256
+
+    def forward(fld, ch):
+        part = jnp.concatenate([fld[ch * GPC + gg].astype(BF16) for gg in range(GPC)], axis=1)
+        rows = slice(ch * GPC * L, (ch + 1) * GPC * L)
+        for i in range(POINTS // QC):
+            at_q = slice(i * QC, (i + 1) * QC)
+            v = jnp.dot(part, basis[rows, at_q], preferred_element_type=F32)
+            if ch:
+                v = values[:, at_q] + v
+            if ch < NCH - 1:
+                values[:, at_q] = v
+            else:
+                rate = jnp.concatenate([gro[...]] * (QC // L), axis=1)
+                react[:, at_q] = (v * (rate - (v * v) * (1.0 / 128.0))).astype(BF16)
 
     def diffuse(first_sweep, here, there):
-        for t in range(SWEEPS):
+        for t in range(SWEEPS - 1):
             sw = first_sweep + t
 
-            def one(ch, carry, t=t, sw=sw, here=here, there=there):
+            def one(ch, carry, sw=sw, here=here, there=there):
                 sweep(sw, here, there, ch)
-                if t < SWEEPS - 1:
-                    send_faces(sw + 1, there, ch)
-                else:
-                    lower(there, ch)
+                send_faces(sw + 1, there, ch)
                 return carry
 
             lax.fori_loop(0, NCH, one, 0)
             here, there = there, here
-
-    QC = 256
-
-    def forward():
-        for i in range(POINTS // QC):
-            at_q = slice(i * QC, (i + 1) * QC)
-            v = jnp.dot(low[...], basis[:, at_q], preferred_element_type=F32)
-            rate = jnp.concatenate([gro[...]] * (QC // L), axis=1)
-            react[:, at_q] = (v * (rate - (v * v) * (1.0 / 128.0))).astype(BF16)
+        for ch in range(NCH):
+            sweep(first_sweep + SWEEPS - 1, here, there, ch)
+            forward(there, ch)
 
     def increment(ch):
         cols = slice(ch * GPC * L, (ch + 1) * GPC * L)
@@ -373,14 +379,12 @@
     lax.fori_loop(0, NCH, arrive, 0)
 
     diffuse(0, fld0, fld1)
-    forward()
     for ch in range(NCH):
         inc = increment(ch)
         for gg in range(GPC):
             fld1[ch * GPC + gg] += inc[:, gg * L : (gg + 1) * L]
         send_faces(SWEEPS, fld1, ch)
     diffuse(SWEEPS, fld1, fld0)
-    forward()
 
     patch = cy * 4 + cx
 
@@ -499,7 +503,7 @@
     result = pl.pallas_call(
         kernel,
         out_shape=jax.ShapeDtypeStruct(planes_first.shape, BF16),
-        in_specs=[pl.BlockSpec(memory_space=pltpu.HBM)] * 5,
+        in_specs=[any_spec] * 5,
         out_specs=any_spec,
         scratch_shapes=[
             V((3, L, 1024), F32),
@@ -523,7 +527,7 @@
             V((2 * SWEEPS, NCH, FROWS * GPC, L), BF16),
             V((2 * SWEEPS, NCH, FROWS * GPC, L), BF16),
             V((MODES, POINTS), BF16),
-            V((ROWS, MODES), BF16),
+            V((ROWS, POINTS), F32),
             V((ROWS, POINTS), BF16),
             V((16, HALF, L), BF16),
             V((16, HALF, L), BF16),
@@ -540,7 +544,7 @@
             DMA((4,)),
         ],
         compiler_params=pltpu.CompilerParams(
-            collective_id=0, has_side_effects=True, vmem_limit_bytes=52 * 1024 * 1024
+            collective_id=0, has_side_effects=True, vmem_limit_bytes=58 * 1024 * 1024
         ),
     )(planes_first, diffusivity, growth_rate, mode_table.T, point_index.T)
     return jnp.transpose(result.astype(F32), (1, 0, 2))

time: 75.3 us -> 70 us (0.930)
  Pallas kernels: 70.6 us -> 67.4 us
  local copies, waits for them, and re-layouts: 3.03 us -> 0 us
  other arithmetic: 1.32 us -> 2.45 us
    pallas_call x1, Pallas kernels: 70.6 us -> 67.4 us  [per_device(): pl.pallas_call(kernel, out_shape=jax.ShapeDtypeStruct(planes_first.shape,...]
    unnamed x8 -> x0, local copies, waits for them, and re-layouts: 3.03 us -> none
    transpose x1, other arithmetic: 1.32 us -> 2.45 us  [per_device(): return jnp.transpose(result.astype(F32), (1, 0, 2))]
where the time goes in v3:
time: 70 us; the launch traced here: 69.8 us
  Pallas kernels  67.4 us (96%)
  other arithmetic  2.45 us (4%)
    pallas_call x1, Pallas kernels, per_device(): pl.pallas_call(kernel, out_shape=jax.ShapeDtypeStruct(planes_first.shape,...  67.4 us
    transpose x1, other arithmetic, per_device(): return jnp.transpose(result.astype(F32), (1, 0, 2))  2.45 us

profile of v3, /device:TPU:15, one launch (start us, length us, event | category | flops | bytes accessed | tf_op | source)
XLA Modules:
  0.0 69.8 jit_solution(5736184050323604934)
XLA Ops:
  0.0 67.4 %shard_map.55 = bf16[3,128,1024]{2,1,0:T(8,128)(2,1)} custom-call(f32[3,128,1024]{2,1,0:T(8,128)} %bitcast.5, f32[3,1024]{1,0:T(4,128)} %dif_hbm.1, f32[3,1024]{1,0:T(4,128)} %gro_hbm.1, s32[8,1024]{1,0:T(8,128)} %bitcast.7, s32[8,2048]{1,0:T(8,128)} %bitcast.6), custom_call_target="tpu_custom_call" | custom-call | tf_op jit(solution)/shard_map/pallas_call | solution.py:503
  67.4 2.5 %convert_bitcast_fusion = f32[128,3,1024]{2,0,1:T(8,128)} fusion(bf16[3,128,1024]{2,1,0:T(8,128)(2,1)} %shard_map.55), kind=kLoop, calls=%fused_computation | loop fusion | flops 393216 | bytes 2359296 | tf_op jit(solution)/shard_map/transpose | solution.py:550

commit v4 on v3

--- a/solution.py
+++ b/solution.py
@@ -7,7 +7,7 @@
 from jax.sharding import PartitionSpec as P
 
 MESH = pl.DeviceIdType.MESH
-F32, BF16, I16, I32 = jnp.float32, jnp.bfloat16, jnp.int16, jnp.int32
+F32, BF16, I32 = jnp.float32, jnp.bfloat16, jnp.int32
 MODES = 1024
 POINTS = 2048
 SWEEPS = 3
@@ -22,13 +22,11 @@
 FROWS = 320
 FAR = (2, 1, 3, 0)
 COMBOS = 96
-STEP = 32000.0
-INV_LN2 = 1.4426950408889634
 
 
 def kernel(
     x_hbm, dif_hbm, gro_hbm, mt_hbm, pi_hbm, out_hbm,
-    xs, kg_src, mt, pi, hot, digit, tab, gain, snd, rcv, kg_rcv, kap, gro, cellmap,
+    xs, kg_src, mt, pi, hot, digit, tab, snd, rcv, kg_rcv, kap, gro, cellmap,
     fld0, fld1, edge, nothing, fsnd, frcv, basis, values, react, fin, fin_rcv, done_low,
     in_sem, a_send, a_recv, kg_send, kg_recv, h_send, h_recv, f_send, f_recv, out_sem,
 ):
@@ -86,16 +84,6 @@
 
     for p in range(3):
         loads[p].wait()
-    big = jnp.zeros((L, L), F32)
-    for p in range(3):
-        for b in range(8):
-            big = jnp.maximum(big, jnp.abs(xs[p, :, b * L : (b + 1) * L]))
-    top = jnp.broadcast_to(jnp.max(big, axis=1, keepdims=True), (L, L))
-    level = jnp.ceil(jnp.log(jnp.maximum(top, 1e-30)) * INV_LN2)
-    gain[...] = jnp.exp2(-level) * STEP
-    tag = jnp.transpose(level)[0:16].astype(I32).astype(I16)
-    for d in range(16):
-        snd[d, HALF : HALF + 16, :] = tag
 
     def spread(j, i):
         px, py = (cx + j) % 4, (cy + i) % 4
@@ -115,13 +103,13 @@
         for p in range(3):
             for b in range(2):
                 cols = pl.ds(pl.multiple_of(px * 256 + b * L, L), L)
-                block = jnp.transpose(jnp.round(xs[p, :, cols] * gain[...]))
+                block = jnp.transpose(xs[p, :, cols])
                 for y in range(4):
                     tile = jnp.concatenate(
                         [block[xi * 32 + y * 8 : xi * 32 + y * 8 + 8] for xi in range(4)], axis=0
                     )
                     row = p * 64 + b * 32
-                    snd[y * 4 + px, row : row + 32, :] = tile.astype(I32).astype(I16)
+                    snd[y * 4 + px, row : row + 32, :] = tile
 
     def spread_column(n):
         j = FAR[n]
@@ -264,7 +252,7 @@
 
             def put(f, value):
                 row = OFFS[f] * GPC + gg * FACES[f]
-                fsnd[sw, ch, row : row + FACES[f], :] = value.astype(BF16)
+                fsnd[sw, ch, row : row + FACES[f], :] = value
 
             put(0, jnp.concatenate([fld[g, z * 64 + 56 : z * 64 + 64, :] for z in range(6)], 0))
             put(1, jnp.concatenate([fld[g, z * 64 : z * 64 + 8, :] for z in range(6)], 0))
@@ -301,7 +289,7 @@
 
             def halo(f):
                 row = OFFS[f] * GPC + gg * FACES[f]
-                return frcv[sw, ch, row : row + FACES[f], :].astype(F32)
+                return frcv[sw, ch, row : row + FACES[f], :]
 
             xl, xh, yl, yh, zl, zh = [halo(f) for f in range(6)]
             for z in range(6):
@@ -324,7 +312,7 @@
     QC = 256
 
     def forward(fld, ch):
-        part = jnp.concatenate([fld[ch * GPC + gg].astype(BF16) for gg in range(GPC)], axis=1)
+        part = jnp.concatenate([fld[ch * GPC + gg, 0:ROWS, :].astype(BF16) for gg in range(GPC)], axis=1)
         rows = slice(ch * GPC * L, (ch + 1) * GPC * L)
         for i in range(POINTS // QC):
             at_q = slice(i * QC, (i + 1) * QC)
@@ -365,11 +353,7 @@
             for c in range(2):
                 slot = g * 2 + c
                 pltpu.make_async_copy(rcv.at[slot], rcv.at[slot], a_recv.at[slot]).wait()
-                level = rcv[slot, HALF : HALF + 16, :].astype(I32).astype(F32)[0:1]
-                unit = jnp.exp2(level) * (1.0 / STEP)
-                fld0[g, c * HALF : (c + 1) * HALF, :] = (
-                    rcv[slot, 0:HALF, :].astype(I32).astype(F32) * unit
-                )
+                fld0[g, c * HALF : (c + 1) * HALF, :] = rcv[slot]
             return carry
 
         lax.fori_loop(0, GPC, one, 0)
@@ -382,7 +366,7 @@
     for ch in range(NCH):
         inc = increment(ch)
         for gg in range(GPC):
-            fld1[ch * GPC + gg] += inc[:, gg * L : (gg + 1) * L]
+            fld1[ch * GPC + gg, 0:ROWS, :] += inc[:, gg * L : (gg + 1) * L]
         send_faces(SWEEPS, fld1, ch)
     diffuse(SWEEPS, fld1, fld0)
 
@@ -408,7 +392,7 @@
         inc = increment(ch)
         for gg in range(GPC):
             g = ch * GPC + gg
-            done = (fld0[g] + inc[:, gg * L : (gg + 1) * L]).astype(BF16)
+            done = (fld0[g, 0:ROWS, :] + inc[:, gg * L : (gg + 1) * L]).astype(BF16)
             for c in range(2):
                 fin[g * 2 + c] = done[c * HALF : (c + 1) * HALF]
 
@@ -420,6 +404,41 @@
                 def _():
                     home(g, c).start()
 
+
+    @pl.when(core != yhi)
+    def _():
+        spread(0, 0).wait_send()
+        coeff(yhi).wait_send()
+        coeff(1 - yhi).wait_send()
+
+    @pl.when(core == yhi)
+    def _():
+        coeff(1 - yhi).wait_send()
+
+    def spread_done(k, carry):
+        spread(k // 4, k % 4).wait_send()
+        return carry
+
+    lax.fori_loop(1, 16, spread_done, 0)
+
+    def faces_done(sw, carry):
+        def sent(f, lo, hi):
+            part = fsnd.at[sw, :, pl.ds(lo * GPC, (hi - lo) * GPC)]
+            pltpu.make_async_copy(part, part, h_send.at[sw, f]).wait()
+
+        sent(0, 0, 192)
+
+        @pl.when(jnp.logical_not(last_plane))
+        def _():
+            sent(1, 192, 256)
+
+        @pl.when(jnp.logical_not(first_plane))
+        def _():
+            sent(2, 256, 320)
+
+        return carry
+
+    lax.fori_loop(0, 2 * SWEEPS, faces_done, 0)
 
     def out_copy(px):
         cols = pl.ds(pl.multiple_of(px * 256, 256), 256)
@@ -445,41 +464,6 @@
         return carry
 
     lax.fori_loop(0, 4, collect, 0)
-
-    @pl.when(core != yhi)
-    def _():
-        spread(0, 0).wait_send()
-        coeff(yhi).wait_send()
-        coeff(1 - yhi).wait_send()
-
-    @pl.when(core == yhi)
-    def _():
-        coeff(1 - yhi).wait_send()
-
-    def spread_done(k, carry):
-        spread(k // 4, k % 4).wait_send()
-        return carry
-
-    lax.fori_loop(1, 16, spread_done, 0)
-
-    def faces_done(sw, carry):
-        def sent(f, lo, hi):
-            part = fsnd.at[sw, :, pl.ds(lo * GPC, (hi - lo) * GPC)]
-            pltpu.make_async_copy(part, part, h_send.at[sw, f]).wait()
-
-        sent(0, 0, 192)
-
-        @pl.when(jnp.logical_not(last_plane))
-        def _():
-            sent(1, 192, 256)
-
-        @pl.when(jnp.logical_not(first_plane))
-        def _():
-            sent(2, 256, 320)
-
-        return carry
-
-    lax.fori_loop(0, 2 * SWEEPS, faces_done, 0)
 
     def home_done(i, carry):
         g, c = i // 2, i % 2
@@ -513,19 +497,18 @@
             V((2, MODES, 256), BF16),
             V((4, COMBOS, 256), I32),
             V((2, 256, 256), BF16),
-            V((L, L), F32),
-            V((16, HALF + 16, L), I16),
-            V((16, HALF + 16, L), I16),
+            V((16, HALF, L), F32),
+            V((16, HALF, L), F32),
             V((2, 2, 3, 1024), F32),
             V((ROWS, L), F32),
             V((ROWS, L), F32),
             V((L, L), F32),
-            V((GROUPS, ROWS, L), F32),
-            V((GROUPS, ROWS, L), F32),
-            V((GPC, ROWS, L), F32),
-            V((64 * GPC, L), BF16),
-            V((2 * SWEEPS, NCH, FROWS * GPC, L), BF16),
-            V((2 * SWEEPS, NCH, FROWS * GPC, L), BF16),
+            V((GROUPS, ROWS + 8, L), F32),
+            V((GROUPS, ROWS + 8, L), F32),
+            V((GPC, ROWS + 8, L), F32),
+            V((64 * GPC, L), F32),
+            V((2 * SWEEPS, NCH, FROWS * GPC, L), F32),
+            V((2 * SWEEPS, NCH, FROWS * GPC, L), F32),
             V((MODES, POINTS), BF16),
             V((ROWS, POINTS), F32),
             V((ROWS, POINTS), BF16),

time: 70 us -> 84.4 us (1.21)
  the two profiles are of different devices: /device:TPU:15 before, /device:TPU:239 now
where the time goes in v4:
time: 84.4 us; the launch traced here: 84.2 us
  Pallas kernels  81.8 us (97%)
  other arithmetic  2.45 us (3%)
    pallas_call x1, Pallas kernels, per_device(): pl.pallas_call(kernel, out_shape=jax.ShapeDtypeStruct(planes_first.shape,...  81.8 us
    transpose x1, other arithmetic, per_device(): return jnp.transpose(result.astype(F32), (1, 0, 2))  2.45 us

profile of v4, /device:TPU:239, one launch (start us, length us, event | category | flops | bytes accessed | tf_op | source)
XLA Modules:
  0.0 84.2 jit_solution(10615838808897199633)
XLA Ops:
  0.0 81.8 %shard_map.55 = bf16[3,128,1024]{2,1,0:T(8,128)(2,1)} custom-call(f32[3,128,1024]{2,1,0:T(8,128)} %bitcast.5, f32[3,1024]{1,0:T(4,128)} %dif_hbm.1, f32[3,1024]{1,0:T(4,128)} %gro_hbm.1, s32[8,1024]{1,0:T(8,128)} %bitcast.7, s32[8,2048]{1,0:T(8,128)} %bitcast.6), custom_call_target="tpu_custom_call" | custom-call | tf_op jit(solution)/shard_map/pallas_call | solution.py:487
  81.8 2.5 %convert_bitcast_fusion = f32[128,3,1024]{2,0,1:T(8,128)} fusion(bf16[3,128,1024]{2,1,0:T(8,128)(2,1)} %shard_map.55), kind=kLoop, calls=%fused_computation | loop fusion | flops 393216 | bytes 2359296 | tf_op jit(solution)/shard_map/transpose | solution.py:533
